TPU v7x, 512 devices: a whole 4x8x8 slice. The times are simulated.
512 devices in a mesh: dp: 8 (over z), expert: 64 (over x, y, core).
Axes of the slice: x: 4, y: 8, z: 8, core: 2. Of those that a mesh axis runs over, the one named last changes fastest.
Arguments:
- tokens: bfloat16 [65536, 1024], P(('dp', 'expert')), may hold values from -6 to 6
- cotangent: bfloat16 [65536, 1024], P(('dp', 'expert')), may hold values from -6 to 6
- routes: int32 [65536, 8], P(('dp', 'expert')), may hold values from 0 to 63, as said below
- combine: float32 [65536, 8], P(('dp', 'expert')), may hold values from 0.1 to 0.5
- w_gate: bfloat16 [64, 1024, 384], P('expert', 'dp'), may hold values from -0.1875 to 0.1875
- w_up: bfloat16 [64, 1024, 384], P('expert', 'dp'), may hold values from -0.1875 to 0.1875
- w_down: bfloat16 [64, 384, 1024], P('expert', None, 'dp'), may hold values from -0.3125 to 0.3125
Outputs:
- mixed: bfloat16 [65536, 1024], P(('dp', 'expert'))
- input_grad: bfloat16 [65536, 1024], P(('dp', 'expert'))
- combine_grad: float32 [65536, 8], P(('dp', 'expert'))
Inputs may be any that keep to these rules, and one draw needn't show every extreme that they name: `routes`: each row names 8 different experts. Among the rows of one device (aligned blocks of 128 rows) each of 2 frequent experts, the same ones on every device, is named by 48 to 56 rows, and every other expert by at most 15 rows, with the counts of the other experts on one device differing by at most one. In every draw some device has a frequent expert named by exactly 56 rows and some device an other expert named by exactly 15 rows.
All inputs are finite; a program needn't handle non-finite values.
Results may differ from a plain program's by a relative error of at most 0.017.
Values may be sent and summed in bfloat16 or wider, within the bound.
No kernel may reach another device: no remote copies, remote signals or barrier semaphores. Data moves between devices by JAX's collectives and lax.ppermute only.
A program may use at most 128 MiB of HBM per device.

v0:
```python
import jax
import jax.numpy as jnp
from jax import lax
from jax.sharding import PartitionSpec as P

HOT = 2


def broadcast(block, axis, owner):
    block = jnp.where(lax.axis_index(axis) == owner, block, jnp.zeros_like(block))
    return lax.psum(block, axis)


def to_owner(array, owners, local_count):
    shape = array.shape
    grouped = array.reshape((owners, local_count) + shape[1:])
    grouped = jnp.swapaxes(grouped, 0, 1)
    return grouped.reshape((local_count, owners * shape[1]) + shape[2:])


def from_owner(array, owners, local_count):
    shape = array.shape
    grouped = array.reshape((local_count, owners, shape[1] // owners) + shape[2:])
    grouped = jnp.swapaxes(grouped, 0, 1)
    return grouped.reshape((owners * local_count, shape[1] // owners) + shape[2:])


def expert_block(row_x, row_dy, row_g, w_g, w_u, w_d):
    gate_pre = jnp.einsum("erd,edf->erf", row_x, w_g, preferred_element_type=jnp.float32)
    up_proj = jnp.einsum("erd,edf->erf", row_x, w_u, preferred_element_type=jnp.float32)
    sigmoid_val = jax.nn.sigmoid(gate_pre)
    silu_val = gate_pre * sigmoid_val
    hidden = (silu_val * up_proj).astype(jnp.bfloat16)
    expert_out = jnp.einsum("erf,efd->erd", hidden, w_d, preferred_element_type=jnp.float32).astype(
        jnp.bfloat16
    )
    dot_grad = jnp.einsum("erd,efd->erf", row_dy, w_d, preferred_element_type=jnp.float32)
    hidden_grad = row_g[:, :, None] * dot_grad
    gate_grad = (
        hidden_grad * up_proj * sigmoid_val * (1.0 + gate_pre * (1.0 - sigmoid_val))
    ).astype(jnp.bfloat16)
    up_grad = (hidden_grad * silu_val).astype(jnp.bfloat16)
    row_grad = jnp.einsum("erf,edf->erd", gate_grad, w_g, preferred_element_type=jnp.float32)
    row_grad = (
        row_grad + jnp.einsum("erf,edf->erd", up_grad, w_u, preferred_element_type=jnp.float32)
    ).astype(jnp.bfloat16)
    return (expert_out, row_grad)


def on_device(tokens, cotangent, routes, combine, w_gate, w_up, w_down):
    tok_rows, width = tokens.shape
    topk = routes.shape[1]
    owners = lax.axis_size("expert")
    local_count = w_gate.shape[0]
    experts = local_count * owners
    pairs = tok_rows * topk
    hot_most = min(tok_rows, 7 * pairs // (2 * experts))
    hot_least = min(tok_rows * 3 // 4, 3 * pairs // experts)
    capacity = (pairs - HOT * hot_least + experts - HOT - 1) // (experts - HOT)
    cold_rows = experts * capacity
    pool_rows = cold_rows + HOT * hot_most
    expert_ids = routes.reshape(-1)
    one_hot = (expert_ids[:, None] == jnp.arange(experts, dtype=jnp.int32)[None, :]).astype(
        jnp.int32
    )
    rank_in = jnp.sum((jnp.cumsum(one_hot, axis=0) - 1) * one_hot, axis=1)
    counts = jnp.sum(one_hot, axis=0)
    top_counts, top_ids = lax.top_k(counts, HOT)
    hot_list = jnp.sort(top_ids)
    match = expert_ids[:, None] == hot_list[None, :]
    is_hot = jnp.any(match, axis=1)
    hot_rank = (
        jnp.sum(jnp.where(match, jnp.arange(HOT, dtype=jnp.int32)[None, :] * hot_most, 0), axis=1)
        + rank_in
    )
    slot_index = jnp.where(is_hot, cold_rows + hot_rank, expert_ids * capacity + rank_in)
    token_index = jnp.arange(pairs, dtype=jnp.int32) // topk
    source_token = jnp.full((pool_rows,), tok_rows, jnp.int32).at[slot_index].set(token_index)
    source_pair = (
        jnp.full((pool_rows,), pairs, jnp.int32)
        .at[slot_index]
        .set(jnp.arange(pairs, dtype=jnp.int32))
    )
    pool_x = jnp.take(tokens, source_token, axis=0, mode="fill", fill_value=0)
    pool_dy = jnp.take(cotangent, source_token, axis=0, mode="fill", fill_value=0)
    pool_g = jnp.take(combine.reshape(-1), source_pair, axis=0, mode="fill", fill_value=0)
    send_x = pool_x[:cold_rows].reshape(experts, capacity, width)
    send_dy = pool_dy[:cold_rows].reshape(experts, capacity, width)
    send_g = pool_g[:cold_rows].reshape(experts, capacity)
    hot_x = pool_x[cold_rows:].reshape(HOT, hot_most, width)
    hot_dy = pool_dy[cold_rows:].reshape(HOT, hot_most, width)
    hot_g = pool_g[cold_rows:].reshape(HOT, hot_most)
    recv_x, recv_dy, recv_g = (
        lax.all_to_all(send_x, "expert", split_axis=0, concat_axis=0, tiled=True),
        lax.all_to_all(send_dy, "expert", split_axis=0, concat_axis=0, tiled=True),
        lax.all_to_all(
            send_g.astype(jnp.bfloat16), "expert", split_axis=0, concat_axis=0, tiled=True
        ).astype(send_g.dtype),
    )
    full_gate, full_up, full_down = (
        lax.all_gather(w_gate, "dp", axis=1, tiled=True),
        lax.all_gather(w_up, "dp", axis=1, tiled=True),
        lax.all_gather(w_down, "dp", axis=2, tiled=True),
    )
    gate_list = []
    up_list = []
    down_list = []
    for which in range(HOT):
        root = hot_list[which] // local_count
        local_slot = hot_list[which] % local_count
        piece_gate = lax.dynamic_index_in_dim(w_gate, local_slot, 0, keepdims=False)
        piece_up = lax.dynamic_index_in_dim(w_up, local_slot, 0, keepdims=False)
        piece_down = lax.dynamic_index_in_dim(w_down, local_slot, 0, keepdims=False)
        shard_gate, shard_up, shard_down = (
            broadcast(piece_gate, "expert", root),
            broadcast(piece_up, "expert", root),
            broadcast(piece_down, "expert", root),
        )
        got_gate, got_up, got_down = (
            lax.all_gather(shard_gate, "dp", axis=0, tiled=True),
            lax.all_gather(shard_up, "dp", axis=0, tiled=True),
            lax.all_gather(shard_down, "dp", axis=1, tiled=True),
        )
        gate_list.append(got_gate)
        up_list.append(got_up)
        down_list.append(got_down)
    hot_out, hot_grad = expert_block(
        hot_x, hot_dy, hot_g, jnp.stack(gate_list), jnp.stack(up_list), jnp.stack(down_list)
    )
    row_x = to_owner(recv_x, owners, local_count)
    row_dy = to_owner(recv_dy, owners, local_count)
    row_g = to_owner(recv_g, owners, local_count)
    expert_out, row_grad = expert_block(row_x, row_dy, row_g, full_gate, full_up, full_down)
    back_out, back_grad = (
        lax.all_to_all(
            from_owner(expert_out, owners, local_count),
            "expert",
            split_axis=0,
            concat_axis=0,
            tiled=True,
        ),
        lax.all_to_all(
            from_owner(row_grad, owners, local_count),
            "expert",
            split_axis=0,
            concat_axis=0,
            tiled=True,
        ),
    )
    pool_out = jnp.concatenate(
        [back_out.reshape(cold_rows, width), hot_out.reshape(HOT * hot_most, width)], axis=0
    )
    pool_grad = jnp.concatenate(
        [back_grad.reshape(cold_rows, width), hot_grad.reshape(HOT * hot_most, width)], axis=0
    )
    out_pairs = pool_out[slot_index].reshape(tok_rows, topk, width)
    grad_pairs = pool_grad[slot_index].reshape(tok_rows, topk, width)
    mixed = jnp.einsum("tk,tkd->td", combine, out_pairs.astype(jnp.float32)).astype(jnp.bfloat16)
    input_grad = jnp.sum(grad_pairs.astype(jnp.float32), axis=1).astype(jnp.bfloat16)
    combine_grad = jnp.einsum(
        "tkd,td->tk", out_pairs, cotangent, preferred_element_type=jnp.float32
    )
    return (mixed, input_grad, combine_grad)


def solution(mesh):
    placed = (
        P(("dp", "expert"), None),
        P(("dp", "expert"), None),
        P(("dp", "expert"), None),
        P(("dp", "expert"), None),
        P("expert", "dp", None),
        P("expert", "dp", None),
        P("expert", None, "dp"),
    )
    return jax.shard_map(
        on_device,
        mesh=mesh,
        in_specs=placed,
        out_specs=(P(("dp", "expert"), None), P(("dp", "expert"), None), P(("dp", "expert"), None)),
        check_vma=False,
    )
```

profile of v0, /device:TPU:22, one launch (start us, length us, event | category | flops | bytes accessed | tf_op | source)
XLA Modules:
  0.0 678.3 jit_solution(17495965251228169367)
XLA Ops:
  10.0 18.0 %reduce-window.6 = s32[64,8,128]{2,1,0:T(8,128)S(1)} reduce-window(s32[64,8,128]{2,1,0:T(8,128)S(1)} %fusion.22, s32[]{:T(128)} %constant.105.clone.1), window={size=1x1x128 pad=0_0x0_0x127_0}, to_apply=%region_5.6 | reduce-window | flops 8323072 | bytes 524292 | tf_op jit(solution)/shard_map/reduce-window
  28.7 2.0 top_k.11
  31.9 4.3 scatter_custom_fusion.1
  36.2 4.4 gather_fusion.1
  41.4 10.6 %all-to-all-start.2 = ((bf16[64,1,15]{2,1,0:T(2,128)(2,1)}), bf16[64,1,15]{2,1,0:T(2,128)(2,1)S(1)}, u32[]{:S(2)}, u32[]{:S(2)}) async-start(bf16[64,1,15]{2,1,0:T(2,128)(2,1)} %convert_element_type.86), calls=%async_computation.2 | async-start | bytes 65536 | tf_op jit(solution)/shard_map/all_to_all | solution.py:96
  52.0 4.3 scatter_custom_fusion
  56.4 4.4 gather_fusion.4
  60.8 4.9 gather_fusion.3
  65.7 3.3 broadcast_select_fusion
  69.1 1.4 copy-done.2
  70.6 1.7 reshape.219
  72.9 10.6 %all-to-all-start = ((bf16[64,15,1024]{2,1,0:T(8,128)(2,1)}), bf16[64,15,1024]{2,1,0:T(8,128)(2,1)}, u32[]{:S(2)}, u32[]{:S(2)}) async-start(bf16[64,15,1024]{2,1,0:T(8,128)(2,1)} %reshape.219), calls=%async_computation | async-start | bytes 4194304 | tf_op jit(solution)/shard_map/all_to_all | solution.py:94
  83.5 1.4 slice.60
  85.0 3.7 reshape.229
  88.7 43.9 %all-to-all-done = bf16[64,15,1024]{2,1,0:T(8,128)(2,1)} async-done(((bf16[64,15,1024]{2,1,0:T(8,128)(2,1)}), bf16[64,15,1024]{2,1,0:T(8,128)(2,1)}, u32[]{:S(2)}, u32[]{:S(2)}) %all-to-all-start) | async-done | bytes 1966112 | tf_op jit(solution)/shard_map/all_to_all | solution.py:94
  132.7 8.0 %all-to-all-start.3 = ((bf16[64,15,1024]{2,1,0:T(8,128)(2,1)}), bf16[64,15,1024]{2,1,0:T(8,128)(2,1)}, u32[]{:S(2)}, u32[]{:S(2)}) async-start(bf16[64,15,1024]{2,1,0:T(8,128)(2,1)} %reshape.229), calls=%async_computation.3 | async-start | bytes 4194304 | tf_op jit(solution)/shard_map/all_to_all | solution.py:95
  140.7 34.4 %all_gather.27 = bf16[1,1024,384]{2,1,0:T(8,128)(2,1)} all-gather(bf16[1,128,384]{2,1,0:T(8,128)(2,1)S(1)} %copy-done.11), channel_id=1, replica_groups=mesh['dp'=8,'expert'=64] {'dp'}, dimensions={1}, use_global_device_ids=true | all-gather | bytes 884736 | tf_op jit(solution)/shard_map/all_gather | solution.py:101
  175.2 26.3 %all_gather.28 = bf16[1,1024,384]{2,1,0:T(8,128)(2,1)S(1)} all-gather(bf16[1,128,384]{2,1,0:T(8,128)(2,1)S(1)} %copy-done.9), channel_id=1, replica_groups=mesh['dp'=8,'expert'=64] {'dp'}, dimensions={1}, use_global_device_ids=true | all-gather | bytes 884736 | tf_op jit(solution)/shard_map/all_gather | solution.py:102
  201.5 27.0 %all_gather.29 = bf16[1,384,1024]{2,1,0:T(8,128)(2,1)} all-gather(bf16[1,384,128]{2,1,0:T(8,128)(2,1)S(1)} %copy-done.10), channel_id=1, replica_groups=mesh['dp'=8,'expert'=64] {'dp'}, dimensions={2}, use_global_device_ids=true | all-gather | bytes 884736 | tf_op jit(solution)/shard_map/all_gather | solution.py:103
  228.5 3.7 reshape.220
  232.2 3.0 fusion.16
  236.5 1.2 copy-done.22
  237.7 2.5 convolution_convert_fusion
  240.2 3.8 reshape_transpose_reshape.8
  244.0 10.4 %all-to-all-start.1 = ((bf16[64,15,1024]{2,1,0:T(8,128)(2,1)}), bf16[64,15,1024]{2,1,0:T(8,128)(2,1)}, u32[]{:S(2)}, u32[]{:S(2)}) async-start(bf16[64,15,1024]{2,1,0:T(8,128)(2,1)} %reshape_transpose_reshape.8), calls=%async_computation.1 | async-start | bytes 4194304 | tf_op jit(solution)/shard_map/all_to_all | solution.py:135
  254.5 1.3 fusion.49
  262.7 193.6 %all-reduce.3.cloned.1.call-done = (bf16[384,128]{1,0:T(8,128)(2,1)}, bf16[384,128]{1,0:T(8,128)(2,1)}, bf16[128,384]{1,0:T(8,128)(2,1)}, bf16[128,384]{1,0:T(8,...) async-done(((bf16[384,128]{1,0:T(8,128)(2,1)}, bf16[384,128]{1,0:T(8,128)(2,1)}, bf16[128,384]{1,0:T(8,128)(2,1)}, bf16[128,384]{1,0:T(8,128)(2,1)}, ...) | async-done | bytes 589840 | tf_op jit(solution)/shard_map/psum | solution.py:11
  456.2 30.5 %all_gather.31 = bf16[1024,384]{1,0:T(8,128)(2,1)} all-gather(bf16[128,384]{1,0:T(8,128)(2,1)} %get-tuple-element.17), channel_id=1, replica_groups=mesh['dp'=8,'expert'=64] {'dp'}, dimensions={0}, use_global_device_ids=true | all-gather | bytes 884736 | tf_op jit(solution)/shard_map/all_gather | solution.py:120
  486.7 2.6 reshape.230
  489.4 2.5 convolution_multiply_fusion
  491.9 1.5 fusion.14
  493.4 1.2 add_convert_fusion
  494.6 1.6 reshape_transpose_reshape.9
  496.3 11.2 %all-to-all-start.4 = ((bf16[64,15,1024]{2,1,0:T(8,128)(2,1)}), bf16[64,15,1024]{2,1,0:T(8,128)(2,1)}, u32[]{:S(2)}, u32[]{:S(2)}) async-start(bf16[64,15,1024]{2,1,0:T(8,128)(2,1)} %reshape_transpose_reshape.9), calls=%async_computation.4 | async-start | bytes 4194304 | tf_op jit(solution)/shard_map/all_to_all | solution.py:142
  507.5 26.3 %all_gather.30 = bf16[1024,384]{1,0:T(8,128)(2,1)S(1)} all-gather(bf16[128,384]{1,0:T(8,128)(2,1)S(1)} %copy-done.17), channel_id=1, replica_groups=mesh['dp'=8,'expert'=64] {'dp'}, dimensions={0}, use_global_device_ids=true | all-gather | bytes 884736 | tf_op jit(solution)/shard_map/all_gather | solution.py:120
  534.2 26.2 %all_gather.33 = bf16[1024,384]{1,0:T(8,128)(2,1)S(1)} all-gather(bf16[128,384]{1,0:T(8,128)(2,1)S(1)} %copy-done.16), channel_id=1, replica_groups=mesh['dp'=8,'expert'=64] {'dp'}, dimensions={0}, use_global_device_ids=true | all-gather | bytes 884736 | tf_op jit(solution)/shard_map/all_gather | solution.py:121
  560.4 26.4 %all_gather.32 = bf16[1024,384]{1,0:T(8,128)(2,1)S(1)} all-gather(bf16[128,384]{1,0:T(8,128)(2,1)S(1)} %copy-done.15), channel_id=1, replica_groups=mesh['dp'=8,'expert'=64] {'dp'}, dimensions={0}, use_global_device_ids=true | all-gather | bytes 884736 | tf_op jit(solution)/shard_map/all_gather | solution.py:121
  587.3 26.6 %all_gather.35 = bf16[384,1024]{1,0:T(8,128)(2,1)S(1)} all-gather(bf16[384,128]{1,0:T(8,128)(2,1)S(1)} %copy-done.14), channel_id=1, replica_groups=mesh['dp'=8,'expert'=64] {'dp'}, dimensions={1}, use_global_device_ids=true | all-gather | bytes 884736 | tf_op jit(solution)/shard_map/all_gather | solution.py:122
  613.9 24.3 %all_gather.34 = bf16[384,1024]{1,0:T(8,128)(2,1)S(1)} all-gather(bf16[384,128]{1,0:T(8,128)(2,1)S(1)} %copy-done.13), channel_id=1, replica_groups=mesh['dp'=8,'expert'=64] {'dp'}, dimensions={1}, use_global_device_ids=true | all-gather | bytes 884736 | tf_op jit(solution)/shard_map/all_gather | solution.py:122
  640.8 3.8 reshape.224
  644.6 1.7 pad_maximum_fusion
  646.3 5.4 gather_fusion
  651.7 2.4 fusion.2
  655.0 1.3 fusion
  656.9 3.7 reshape.231
  660.7 1.7 pad_maximum_fusion.1
  662.4 5.4 gather_fusion.2
  667.8 3.7 bitcast_reduce_fusion
  (106 shorter events, 17.8 us)
Async XLA Ops:
  7.2 49.2 %copy-start = (bf16[128,1024]{1,0:T(8,128)(2,1)S(1)}, bf16[128,1024]{1,0:T(8,128)(2,1)}, u32[]{:S(2)}) copy-start(bf16[128,1024]{1,0:T(8,128)(2,1)} %param.10) | copy-start | bytes 786436
  31.4 0.5 copy-start.19
  41.4 30.9 %all-to-all-start.2 = ((bf16[64,1,15]{2,1,0:T(2,128)(2,1)}), bf16[64,1,15]{2,1,0:T(2,128)(2,1)S(1)}, u32[]{:S(2)}, u32[]{:S(2)}) async-start(bf16[64,1,15]{2,1,0:T(2,128)(2,1)} %convert_element_type.86), calls=%async_computation.2 | async-start | bytes 65536 | tf_op jit(solution)/shard_map/all_to_all | solution.py:96
  56.4 4.4 copy-start.1
  69.1 1.4 copy-start.2
  72.3 11.3 %copy-start.3 = (bf16[1072,1024]{1,0:T(8,128)(2,1)S(1)}, bf16[1072,1024]{1,0:T(8,128)(2,1)}, u32[]{:S(2)}) copy-start(bf16[1072,1024]{1,0:T(8,128)(2,1)} %get-tuple-element.25) | copy-start | bytes 6586372
  72.3 0.6 copy-start.12
  72.9 59.8 %all-to-all-start = ((bf16[64,15,1024]{2,1,0:T(8,128)(2,1)}), bf16[64,15,1024]{2,1,0:T(8,128)(2,1)}, u32[]{:S(2)}, u32[]{:S(2)}) async-start(bf16[64,15,1024]{2,1,0:T(8,128)(2,1)} %reshape.219), calls=%async_computation | async-start | bytes 4194304 | tf_op jit(solution)/shard_map/all_to_all | solution.py:94
  88.7 52.0 %copy-start.11 = (bf16[1,128,384]{2,1,0:T(8,128)(2,1)S(1)}, bf16[1,128,384]{2,1,0:T(8,128)(2,1)}, u32[]{:S(2)}) copy-start(bf16[1,128,384]{2,1,0:T(8,128)(2,1)} %param.13) | copy-start | bytes 294916
  88.7 86.5 %copy-start.9 = (bf16[1,128,384]{2,1,0:T(8,128)(2,1)S(1)}, bf16[1,128,384]{2,1,0:T(8,128)(2,1)}, u32[]{:S(2)}) copy-start(bf16[1,128,384]{2,1,0:T(8,128)(2,1)} %param.14) | copy-start | bytes 294916
  88.7 112.8 %copy-start.10 = (bf16[1,384,128]{2,1,0:T(8,128)(2,1)S(1)}, bf16[1,384,128]{2,1,0:T(8,128)(2,1)}, u32[]{:S(2)}) copy-start(bf16[1,384,128]{2,1,0:T(8,128)(2,1)} %param.15) | copy-start | bytes 294916
  132.7 111.3 %all-to-all-start.3 = ((bf16[64,15,1024]{2,1,0:T(8,128)(2,1)}), bf16[64,15,1024]{2,1,0:T(8,128)(2,1)}, u32[]{:S(2)}, u32[]{:S(2)}) async-start(bf16[64,15,1024]{2,1,0:T(8,128)(2,1)} %reshape.229), calls=%async_computation.3 | async-start | bytes 4194304 | tf_op jit(solution)/shard_map/all_to_all | solution.py:95
  232.2 3.0 copy-start.5
  235.3 1.2 copy-start.20
  235.3 2.4 copy-start.7
  236.5 1.2 copy-start.22
  244.0 252.3 %all-to-all-start.1 = ((bf16[64,15,1024]{2,1,0:T(8,128)(2,1)}), bf16[64,15,1024]{2,1,0:T(8,128)(2,1)}, u32[]{:S(2)}, u32[]{:S(2)}) async-start(bf16[64,15,1024]{2,1,0:T(8,128)(2,1)} %reshape_transpose_reshape.8), calls=%async_computation.1 | async-start | bytes 4194304 | tf_op jit(solution)/shard_map/all_to_all | solution.py:135
  254.4 6.4 copy-start.18
  254.4 201.8 %all-reduce.3.cloned.1.call-start = ((), (), s32[]{:S(2)}) async-start(), calls=%async_computation.5 | async-start | bytes 1179648 | tf_op jit(solution)/shard_map/psum | solution.py:11
  489.3 2.5 copy-start.6
  489.4 2.5 copy-start.21
  489.4 2.5 copy-start.23
  496.3 11.3 %copy-start.17 = (bf16[128,384]{1,0:T(8,128)(2,1)S(1)}, bf16[128,384]{1,0:T(8,128)(2,1)}, u32[]{:S(2)}) copy-start(bf16[128,384]{1,0:T(8,128)(2,1)} %get-tuple-element.18) | copy-start | bytes 294916
  496.3 37.6 %copy-start.8 = (bf16[1024,384]{1,0:T(8,128)(2,1)S(1)}, bf16[1024,384]{1,0:T(8,128)(2,1)}, u32[]{:S(2)}) copy-start(bf16[1024,384]{1,0:T(8,128)(2,1)} %all_gather.31) | copy-start | bytes 2359300
  496.3 160.7 %all-to-all-start.4 = ((bf16[64,15,1024]{2,1,0:T(8,128)(2,1)}), bf16[64,15,1024]{2,1,0:T(8,128)(2,1)}, u32[]{:S(2)}, u32[]{:S(2)}) async-start(bf16[64,15,1024]{2,1,0:T(8,128)(2,1)} %reshape_transpose_reshape.9), calls=%async_computation.4 | async-start | bytes 4194304 | tf_op jit(solution)/shard_map/all_to_all | solution.py:142
  507.5 26.7 %copy-start.16 = (bf16[128,384]{1,0:T(8,128)(2,1)S(1)}, bf16[128,384]{1,0:T(8,128)(2,1)}, u32[]{:S(2)}) copy-start(bf16[128,384]{1,0:T(8,128)(2,1)} %get-tuple-element.15) | copy-start | bytes 294916
  533.8 26.6 %copy-start.15 = (bf16[128,384]{1,0:T(8,128)(2,1)S(1)}, bf16[128,384]{1,0:T(8,128)(2,1)}, u32[]{:S(2)}) copy-start(bf16[128,384]{1,0:T(8,128)(2,1)} %get-tuple-element.16) | copy-start | bytes 294916
  560.4 26.9 %copy-start.14 = (bf16[384,128]{1,0:T(8,128)(2,1)S(1)}, bf16[384,128]{1,0:T(8,128)(2,1)}, u32[]{:S(2)}) copy-start(bf16[384,128]{1,0:T(8,128)(2,1)} %get-tuple-element.13) | copy-start | bytes 294916
  586.8 27.1 %copy-start.13 = (bf16[384,128]{1,0:T(8,128)(2,1)S(1)}, bf16[384,128]{1,0:T(8,128)(2,1)}, u32[]{:S(2)}) copy-start(bf16[384,128]{1,0:T(8,128)(2,1)} %get-tuple-element.14) | copy-start | bytes 294916
  651.7 3.2 copy-start.4
Sparse Core Ops, SparseCore 0:
  259.9 196.3 all-reduce.2
where the time goes:
time: 680 us; the launch traced here: 678 us
  blocking collectives  248 us (36%)
  waiting for transfers between devices  238 us (35%)
  local copies, waits for them, and re-layouts  71.4 us (11%)
  starting transfers between devices  51 us (8%)
  other arithmetic  35.4 us (5%)
  matrix products  19 us (3%)
  between operations  15.9 us (2%)
    psum x1, waiting for transfers between devices, broadcast(): return lax.psum(block, axis)  194 us
    all_gather x2, blocking collectives, on_device(): lax.all_gather(shard_gate, 'dp', axis=0, tiled=True)  56.8 us
    all_gather x2, blocking collectives, on_device(): lax.all_gather(shard_up, 'dp', axis=0, tiled=True)  52.6 us
    all_gather x2, blocking collectives, on_device(): lax.all_gather(shard_down, 'dp', axis=1, tiled=True)  51 us
    all_to_all x1, waiting for transfers between devices, on_device(): lax.all_to_all(send_x, 'expert', split_axis=0, concat_axis=0, tiled=True)  43.9 us
    all_gather x1, blocking collectives, on_device(): lax.all_gather(w_gate, 'dp', axis=1, tiled=True)  34.4 us
    all_gather x1, blocking collectives, on_device(): lax.all_gather(w_down, 'dp', axis=2, tiled=True)  27 us
    all_gather x1, blocking collectives, on_device(): lax.all_gather(w_up, 'dp', axis=1, tiled=True)  26.3 us
  transfers between devices with their start and end apart: 6, of which 2 were waited for; matrix products, arithmetic and copies ran while one was open for 11% of the time, Pallas kernels for 0%

commit v1 on v0

v1 whole, which is shorter than its diff:
```python
import functools

import jax
import jax.numpy as jnp
from jax import lax
from jax.experimental import pallas as pl
from jax.experimental.pallas import tpu as pltpu
from jax.sharding import Mesh, PartitionSpec as P

GROUP = ("x", "core")
CHUNK = 128
META = 128
BF, F32 = jnp.bfloat16, jnp.float32


def nn(a, b):
    return jnp.dot(a, b, preferred_element_type=F32)


def nt(a, b):
    return lax.dot_general(a, b, (((1,), (1,)), ((), ())), preferred_element_type=F32)


def tn(a, b):
    return lax.dot_general(a, b, (((0,), (0,)), ((), ())), preferred_element_type=F32)


def pack(tokens, cotangent, routes, combine):
    high = combine.astype(BF)
    low = (combine - high.astype(F32)).astype(BF)
    pad = jnp.zeros((tokens.shape[0], META - 3 * routes.shape[1]), BF)
    return jnp.concatenate([tokens, cotangent, routes.astype(BF), high, low, pad], axis=1)


def experts_kernel(topk, first_ref, t_ref, w_ref, out_ref, rank_ref, acc_ref):
    step = pl.program_id(0)
    local = pl.num_programs(0)
    rows, wide = t_ref.shape
    width = (wide - META) // 2
    first = first_ref[0]
    stride = first_ref[1]

    @pl.when(step == 0)
    def _():
        acc_ref[...] = jnp.zeros_like(acc_ref)
        routes = t_ref[:, 2 * width :].astype(F32).T[:topk]
        masks = []
        for j in range(local):
            name = (first + j * stride).astype(F32)
            masks.append(jnp.max(jnp.where(routes == name, 1.0, 0.0), axis=0, keepdims=True))
        mask = jnp.concatenate(masks, axis=0)
        before = lax.broadcasted_iota(jnp.int32, (rows, rows), 0) < lax.broadcasted_iota(
            jnp.int32, (rows, rows), 1
        )
        rank = nn(mask.astype(BF), jnp.where(before, 1.0, 0.0).astype(BF))
        rank_ref[...] = jnp.where(mask > 0, rank, -1.0)

    rank = rank_ref[pl.ds(step, 1), :]
    count = jnp.max(rank).astype(jnp.int32) + 1
    name = (first + step * stride).astype(F32)
    depth = w_ref.shape[0] * w_ref.shape[3]

    def weight(which):
        return w_ref[:, 0, which].reshape(depth, w_ref.shape[4])

    def chunk(c, carry):
        slot = (lax.broadcasted_iota(jnp.int32, (CHUNK, rows), 0) + c * CHUNK).astype(F32)
        pick = jnp.where(rank == slot, 1.0, 0.0).astype(BF)
        x = nn(pick, t_ref[:, :width]).astype(BF)
        dy = nn(pick, t_ref[:, width : 2 * width]).astype(BF)
        meta = nn(pick, t_ref[:, 2 * width :])
        lane = lax.broadcasted_iota(jnp.int32, meta.shape, 1)
        hit = (meta == name) & (lane < topk)
        both = pltpu.roll(meta, META - topk, 1) + pltpu.roll(meta, META - 2 * topk, 1)
        g = jnp.sum(jnp.where(hit, both, 0.0), axis=1, keepdims=True)
        gate = nn(x, weight(0))
        up = nn(x, weight(1))
        sig = jax.nn.sigmoid(gate)
        silu = gate * sig
        hidden = (silu * up).astype(BF)
        hidden_grad = g * nn(dy, weight(2))
        gate_grad = (hidden_grad * up * sig * (1.0 + gate * (1.0 - sig))).astype(BF)
        up_grad = (hidden_grad * silu).astype(BF)
        eo = nt(hidden, weight(2)).astype(BF).astype(F32)
        grad = (nt(gate_grad, weight(0)) + nt(up_grad, weight(1))).astype(BF)
        cg = jnp.sum(eo * dy.astype(F32), axis=1, keepdims=True)
        cg_high = cg.astype(BF).astype(F32)
        tail = jnp.where(hit, cg_high, 0.0) + pltpu.roll(jnp.where(hit, cg - cg_high, 0.0), topk, 1)
        acc_ref[:, :width] += tn(pick, (g * eo).astype(BF))
        acc_ref[:, width : 2 * width] += tn(pick, grad)
        acc_ref[:, 2 * width :] += tn(pick, tail.astype(BF))
        return carry

    lax.fori_loop(0, (count + CHUNK - 1) // CHUNK, chunk, 0)

    @pl.when(step == local - 1)
    def _():
        out_ref[...] = acc_ref[...].astype(BF)


def experts(first, packed, weights, topk):
    zs, local, three, part, hidden = weights.shape
    rows, wide = packed.shape
    return pl.pallas_call(
        functools.partial(experts_kernel, topk),
        grid_spec=pltpu.PrefetchScalarGridSpec(
            num_scalar_prefetch=1,
            grid=(local,),
            in_specs=[
                pl.BlockSpec((rows, wide), lambda i, s: (0, 0)),
                pl.BlockSpec((zs, 1, three, part, hidden), lambda i, s: (0, i, 0, 0, 0)),
            ],
            out_specs=pl.BlockSpec((rows, wide), lambda i, s: (0, 0)),
            scratch_shapes=[pltpu.VMEM((local, rows), F32), pltpu.VMEM((rows, wide), F32)],
        ),
        out_shape=jax.ShapeDtypeStruct((rows, wide), BF),
        compiler_params=pltpu.CompilerParams(vmem_limit_bytes=56 * 1024 * 1024),
    )(first, packed, weights)


def on_device(tokens, cotangent, routes, combine, w_gate, w_up, w_down):
    rows, width = tokens.shape
    topk = routes.shape[1]
    members = lax.axis_size("x") * lax.axis_size("core")
    shard = jnp.stack([w_gate[0], w_up[0], w_down[0].T])
    weights = lax.all_gather(shard, ("dp", "y"), axis=0)
    weights = weights.reshape((lax.axis_size("dp"), lax.axis_size("y")) + shard.shape)
    packed = lax.all_gather(pack(tokens, cotangent, routes, combine), GROUP, axis=0, tiled=True)
    cores = lax.axis_size("core")
    first = lax.axis_index("x") * lax.axis_size("y") * cores + lax.axis_index("core")
    partial = experts(jnp.stack([first, jnp.full_like(first, cores)]), packed, weights, topk)
    partial = partial.reshape(members, rows, packed.shape[1])
    mine = lax.psum_scatter(partial, GROUP, scatter_dimension=0)
    tail = mine[:, 2 * width :].astype(F32)
    return mine[:, :width], mine[:, width : 2 * width], tail[:, :topk] + tail[:, topk : 2 * topk]


def solution(mesh):
    split = Mesh(mesh.devices.reshape(8, 4, 8, 2), ("dp", "x", "y", "core"))
    owner = ("x", "y", "core")
    token = P(("dp",) + owner, None)
    return jax.shard_map(
        on_device,
        mesh=split,
        in_specs=(token,) * 4 + (P(owner, "dp", None), P(owner, "dp", None), P(owner, None, "dp")),
        out_specs=(token, token, token),
        check_vma=False,
    )
```

time: 680 us -> 307 us (0.45)
  the two profiles are of different devices: /device:TPU:22 before, /device:TPU:1 now
where the time goes in v1:
time: 307 us; the launch traced here: 305 us
  waiting for transfers between devices  232 us (76%)
  Pallas kernels  41.8 us (14%)
  between operations  13.8 us (4%)
  local copies, waits for them, and re-layouts  12.5 us (4%)
  other arithmetic  5.1 us (2%)
    all_gather x1, waiting for transfers between devices, on_device(): weights = lax.all_gather(shard, ('dp', 'y'), axis=0)  153 us
    pallas_call x1, Pallas kernels, experts(): pl.pallas_call(functools.partial(experts_kernel, topk), grid_spec=pltpu.P...  41.8 us
    all_gather x1, waiting for transfers between devices, on_device(): lax.all_gather(pack(tokens, cotangent, routes, combine), GROUP, axis=0, t...  41.2 us
    reduce_scatter x1, waiting for transfers between devices, on_device(): mine = lax.psum_scatter(partial, GROUP, scatter_dimension=0)  38.2 us
    reshape x1, local copies, waits for them, and re-layouts, on_device(): partial = partial.reshape(members, rows, packed.shape[1])  6.4 us
  transfers between devices with their start and end apart: 3, of which 3 were waited for; matrix products, arithmetic and copies ran while one was open for 1% of the time, Pallas kernels for 0%

profile of v1, /device:TPU:1, one launch (start us, length us, event | category | flops | bytes accessed | tf_op | source)
XLA Modules:
  0.0 305.4 jit_solution(13748260003786100780)
XLA Ops:
  7.2 0.0 all-gather.4.cloned.1.call-start
  7.2 0.7 convert_element_type.15
  7.9 0.8 subtract_convert_fusion
  8.7 0.1 copy.21
  8.8 0.1 copy.19
  8.9 0.1 copy.20
  9.1 1.9 concatenate.3
  11.0 0.0 all-gather.4.cloned.1.call-update
  11.0 0.0 all-gather.6.cloned.1.call-start
  11.0 1.0 copy.22
  12.0 1.7 pad_maximum_fusion
  13.7 0.0 all-gather.6.cloned.1.call-update
  13.8 0.0 reduce-scatter.2.cloned.1.call-start
  13.8 0.6 pad_add_fusion.first_ref
  14.4 41.2 %all-gather.4.cloned.1.call-done.t_ref = bf16[1024,2176]{1,0:T(8,128)(2,1)} async-done(((bf16[128,2176]{1,0:T(8,128)(2,1)}), bf16[1024,2176]{1,0:T(8,128)(2,1)}) %all-gather.4.cloned.1.call-update) | async-done | bytes 4456464 | tf_op jit(solution)/shard_map/all_gather | solution.py:128
  55.6 152.8 %all-gather.6.cloned.1.call-done = bf16[192,128,384]{2,1,0:T(8,128)(2,1)} async-done(((bf16[3,128,384]{2,1,0:T(8,128)(2,1)}), bf16[192,128,384]{2,1,0:T(8,128)(2,1)}) %all-gather.6.cloned.1.call-update) | async-done | bytes 18874384 | tf_op jit(solution)/shard_map/all_gather | solution.py:126
  208.4 41.8 %shard_map.94 = bf16[1024,2176]{1,0:T(8,128)(2,1)} custom-call(s32[2]{0:T(128)} %pad_add_fusion.first_ref, bf16[1024,2176]{1,0:T(8,128)(2,1)} %all-gather.4.cloned.1.call-done.t_ref, bf16[8,8,3,128,384]{4,3,2,1,0:T(8,128)(2,1)} %bitcast.9), custom_call_target="tpu_custom_call" | custom-call | tf_op jit(solution)/shard_map/pallas_call | solution.py:104
  250.2 6.4 %copy.23 = bf16[8,128,2176]{1,2,0:T(8,128)(2,1)} copy(bf16[8,128,2176]{2,1,0:T(8,128)(2,1)} %bitcast.10) | data formatting | bytes 8912896 | tf_op jit(solution)/shard_map/reshape | solution.py:132
  256.6 0.0 reduce-scatter.2.cloned.1.call-update
  256.6 38.2 %reduce-scatter.2.cloned.1.call-done = bf16[1,128,2176]{1,2,0:T(8,128)(2,1)} async-done(((bf16[8,128,2176]{1,2,0:T(8,128)(2,1)}), bf16[1,128,2176]{1,2,0:T(8,128)(2,1)}) %reduce-scatter.2.cloned.1.call-update) | async-done | bytes 557072 | tf_op jit(solution)/shard_map/reduce_scatter | solution.py:133
  294.8 0.8 slice_convert_fusion
  295.5 1.1 fusion
  296.6 0.6 slice_add_fusion
  297.2 0.8 copy.25
  298.0 0.8 copy.24
  (1 shorter events, 0.0 us)
Async XLA Ops:
  7.2 48.4 %all-gather.4.cloned.1.call-start = ((), (), s32[]{:S(2)}) async-start(), calls=%async_computation.1 | async-start | bytes 5013504 | tf_op jit(solution)/shard_map/all_gather | solution.py:128
  11.0 197.4 %all-gather.6.cloned.1.call-start = ((), (), s32[]{:S(2)}) async-start(), calls=%async_computation.3 | async-start | bytes 19169280 | tf_op jit(solution)/shard_map/all_gather | solution.py:126
  13.8 281.0 %reduce-scatter.2.cloned.1.call-start = ((), (), s32[]{:S(2)}) async-start(), calls=%async_computation.2 | async-start | bytes 5013504 | tf_op jit(solution)/shard_map/reduce_scatter | solution.py:133
Sparse Core Ops, SparseCore 0:
  11.1 44.4 all-gather.3
  58.6 149.7 all-gather.5
  256.7 38.0 reduce-scatter.1

commit v2 on v1

v2 whole, which is shorter than its diff:
```python
import functools

import jax
import jax.numpy as jnp
from jax import lax
from jax.experimental import pallas as pl
from jax.experimental.pallas import tpu as pltpu
from jax.sharding import Mesh, PartitionSpec as P

SIZE = 128
SLOTS = 16
CHUNKS = 16
META = 128
BF, F32 = jnp.bfloat16, jnp.float32


def nn(a, b):
    return jnp.dot(a, b, preferred_element_type=F32)


def nt(a, b):
    return lax.dot_general(a, b, (((1,), (1,)), ((), ())), preferred_element_type=F32)


def tn(a, b):
    return lax.dot_general(a, b, (((0,), (0,)), ((), ())), preferred_element_type=F32)


def pack(tokens, cotangent, routes, combine):
    high = combine.astype(BF)
    low = (combine - high.astype(F32)).astype(BF)
    pad = jnp.zeros((tokens.shape[0], META - 3 * routes.shape[1]), BF)
    return jnp.concatenate([tokens, cotangent, routes.astype(BF), high, low, pad], axis=1)


def route_kernel(topk, first_ref, own_ref, other_ref, rows_ref, pick_ref, table_ref, rank_ref):
    local = rank_ref.shape[1]
    blocks, slots, size = pick_ref.shape
    wide = own_ref.shape[1]
    half = blocks // 2
    before = lax.broadcasted_iota(jnp.int32, (size, size), 0) < lax.broadcasted_iota(
        jnp.int32, (size, size), 1
    )
    before = jnp.where(before, 1.0, 0.0).astype(BF)

    def block(b):
        ref = own_ref if b < half else other_ref
        return ref[(b % half) * size : (b % half + 1) * size]

    for b in range(blocks):
        routes = block(b)[:, wide - META :].astype(F32).T[:topk]
        masks = []
        for j in range(local):
            name = (first_ref[0] + j * first_ref[1]).astype(F32)
            masks.append(jnp.max(jnp.where(routes == name, 1.0, 0.0), axis=0, keepdims=True))
        mask = jnp.concatenate(masks, axis=0)
        rank_ref[b] = jnp.where(mask > 0, nn(mask.astype(BF), before), -1.0)
    bases = [jnp.int32(0)]
    for j in range(local):
        count = jnp.max(rank_ref[:, j]).astype(jnp.int32) + 1
        bases.append(bases[j] + (count + SLOTS - 1) // SLOTS)
    chunks = table_ref.shape[0] - 1
    for q in range(chunks):
        at = jnp.int32(0)
        for j in range(local - 1):
            at += (bases[j + 1] <= q).astype(jnp.int32)
        table_ref[q] = at
    table_ref[chunks] = bases[local]
    slot = lax.broadcasted_iota(jnp.int32, (slots, size), 0)
    for b in range(blocks):
        pick = jnp.zeros((slots, size), F32)
        for j in range(local):
            rank = rank_ref[b, j : j + 1]
            where = rank + (bases[j] * SLOTS).astype(F32)
            pick = jnp.where((where == slot.astype(F32)) & (rank >= 0), 1.0, pick)
        pick = pick.astype(BF)
        pick_ref[b] = pick
        rows_ref[:, b] = nn(pick, block(b)).astype(BF).reshape(chunks, SLOTS, wide)


def experts_kernel(topk, first_ref, table_ref, rows_ref, pick_ref, w_ref, own_ref, other_ref, back_ref):
    q = pl.program_id(0)
    chunks = pl.num_programs(0)
    blocks, slots, size = pick_ref.shape
    wide = rows_ref.shape[3]
    width = (wide - META) // 2
    count = blocks * SLOTS
    depth = w_ref.shape[0] * w_ref.shape[3]

    @pl.when(q >= table_ref[chunks])
    def _():
        back_ref[q] = jnp.zeros(back_ref.shape[1:], BF)

    @pl.when(q < table_ref[chunks])
    def _():
        name = (first_ref[0] + table_ref[q] * first_ref[1]).astype(F32)

        def weight(which):
            return w_ref[:, 0, which].reshape(depth, w_ref.shape[4])

        x = rows_ref[0, :, :, :width].reshape(count, width)
        dy = rows_ref[0, :, :, width : 2 * width].reshape(count, width)
        meta = rows_ref[0, :, :, 2 * width :].astype(F32).reshape(count, META)
        lane = lax.broadcasted_iota(jnp.int32, meta.shape, 1)
        hit = (meta == name) & (lane < topk)
        both = pltpu.roll(meta, META - topk, 1) + pltpu.roll(meta, META - 2 * topk, 1)
        g = jnp.sum(jnp.where(hit, both, 0.0), axis=1, keepdims=True)
        gate = nn(x, weight(0))
        up = nn(x, weight(1))
        sig = jax.nn.sigmoid(gate)
        silu = gate * sig
        hidden = (silu * up).astype(BF)
        hidden_grad = g * nn(dy, weight(2))
        gate_grad = (hidden_grad * up * sig * (1.0 + gate * (1.0 - sig))).astype(BF)
        up_grad = (hidden_grad * silu).astype(BF)
        eo = nt(hidden, weight(2)).astype(BF).astype(F32)
        grad = (nt(gate_grad, weight(0)) + nt(up_grad, weight(1))).astype(BF)
        cg = jnp.sum(eo * dy.astype(F32), axis=1, keepdims=True)
        cg_high = cg.astype(BF).astype(F32)
        tail = jnp.where(hit, cg_high, 0.0) + pltpu.roll(jnp.where(hit, cg - cg_high, 0.0), topk, 1)
        cut = (blocks, SLOTS)
        back_ref[q, :, :, :width] = (g * eo).astype(BF).reshape(cut + (width,))
        back_ref[q, :, :, width : 2 * width] = grad.reshape(cut + (width,))
        back_ref[q, :, :, 2 * width :] = tail.astype(BF).reshape(cut + (META,))

    @pl.when(q == chunks - 1)
    def _():
        half = blocks // 2
        for b in range(blocks):
            ref = own_ref if b < half else other_ref
            at = (b % half) * size
            ref[at : at + size] = tn(pick_ref[b], back_ref[:, b].reshape(slots, wide)).astype(BF)


def route(first, own, other, local, topk):
    half, wide = own.shape
    blocks = 2 * half // SIZE
    vmem = pl.BlockSpec(memory_space=pltpu.VMEM)
    smem = pl.BlockSpec(memory_space=pltpu.SMEM)
    return pl.pallas_call(
        functools.partial(route_kernel, topk),
        in_specs=[smem, vmem, vmem],
        out_specs=[vmem, vmem, smem],
        out_shape=[
            jax.ShapeDtypeStruct((CHUNKS, blocks, SLOTS, wide), BF),
            jax.ShapeDtypeStruct((blocks, CHUNKS * SLOTS, SIZE), BF),
            jax.ShapeDtypeStruct((CHUNKS + 1,), jnp.int32),
        ],
        scratch_shapes=[pltpu.VMEM((blocks, local, SIZE), F32)],
        compiler_params=pltpu.CompilerParams(vmem_limit_bytes=40 * 1024 * 1024),
        cost_estimate=pl.CostEstimate(
            flops=2 * 2 * half * CHUNKS * SLOTS * wide, bytes_accessed=18_000_000, transcendentals=0
        ),
    )(first, own, other)


def experts(first, table, rows, pick, weights, topk):
    zs, local, three, part, hidden = weights.shape
    chunks, blocks, slots, wide = rows.shape
    half = blocks * SIZE // 2
    whole = pl.BlockSpec((half, wide), lambda q, s, t: (0, 0))
    return pl.pallas_call(
        functools.partial(experts_kernel, topk),
        grid_spec=pltpu.PrefetchScalarGridSpec(
            num_scalar_prefetch=2,
            grid=(chunks,),
            in_specs=[
                pl.BlockSpec((1, blocks, slots, wide), lambda q, s, t: (q, 0, 0, 0)),
                pl.BlockSpec(pick.shape, lambda q, s, t: (0, 0, 0)),
                pl.BlockSpec((zs, 1, three, part, hidden), lambda q, s, t: (0, t[q], 0, 0, 0)),
            ],
            out_specs=[whole, whole],
            scratch_shapes=[pltpu.VMEM(rows.shape, BF)],
        ),
        out_shape=[jax.ShapeDtypeStruct((half, wide), BF)] * 2,
        compiler_params=pltpu.CompilerParams(vmem_limit_bytes=48 * 1024 * 1024),
        cost_estimate=pl.CostEstimate(
            flops=2 * 6 * CHUNKS * SIZE * 1024 * hidden, bytes_accessed=36_000_000, transcendentals=0
        ),
    )(first, table, rows, pick, weights)


def shift(array, axis, by):
    size = lax.axis_size(axis)
    return lax.ppermute(array, axis, [(i, (i + by) % size) for i in range(size)])


def gather_group(own):
    middle = own.shape[0] // 2
    left, right = shift(own, "x", 1), shift(own, "x", -1)
    far = [shift(left[:middle], "x", 1), shift(right[middle:], "x", -1)]
    mine = jnp.concatenate([own, right] + far + [left], axis=0)
    return mine, shift(mine, "core", 1)


def add(a, b):
    return (a.astype(F32) + b.astype(F32)).astype(BF)


def sum_group(mine, other):
    total = add(mine, shift(other, "core", 1))
    size = total.shape[0] // 4
    middle = size // 2
    part = [total[o * size : (o + 1) * size] for o in range(4)]
    from_left = shift(part[2][:middle], "x", 1)
    from_right = shift(part[2][middle:], "x", -1)
    to_right = jnp.concatenate([add(part[1][:middle], from_left), part[1][middle:]], axis=0)
    to_left = jnp.concatenate([part[3][:middle], add(part[3][middle:], from_right)], axis=0)
    return part[0].astype(F32) + shift(to_right, "x", 1).astype(F32) + shift(to_left, "x", -1).astype(F32)


def on_device(tokens, cotangent, routes, combine, w_gate, w_up, w_down):
    width = tokens.shape[1]
    topk = routes.shape[1]
    shard = jnp.stack([w_gate[0], w_up[0], w_down[0].T])
    weights = lax.all_gather(shard, ("dp", "y"), axis=0)
    weights = weights.reshape((lax.axis_size("dp"), lax.axis_size("y")) + shard.shape)
    mine, other = gather_group(pack(tokens, cotangent, routes, combine))
    cores = lax.axis_size("core")
    first = lax.axis_index("x") * lax.axis_size("y") * cores + lax.axis_index("core")
    first = jnp.stack([first, jnp.full_like(first, cores)])
    rows, pick, table = route(first, mine, other, weights.shape[1], topk)
    total = sum_group(*experts(first, table, rows, pick, weights, topk))
    tail = total[:, 2 * width :]
    return (
        total[:, :width].astype(BF),
        total[:, width : 2 * width].astype(BF),
        tail[:, :topk] + tail[:, topk : 2 * topk],
    )


def solution(mesh):
    split = Mesh(mesh.devices.reshape(8, 4, 8, 2), ("dp", "x", "y", "core"))
    owner = ("x", "y", "core")
    token = P(("dp",) + owner, None)
    return jax.shard_map(
        on_device,
        mesh=split,
        in_specs=(token,) * 4 + (P(owner, "dp", None), P(owner, "dp", None), P(owner, None, "dp")),
        out_specs=(token, token, token),
        check_vma=False,
    )
```

time: 307 us -> 240 us (0.78)
  waiting for transfers between devices: 232 us -> 145 us
  starting transfers between devices: 0.12 us -> 41.7 us
  Pallas kernels: 41.8 us -> 25.4 us
  local copies, waits for them, and re-layouts: 12.5 us -> 8 us
    all_gather x1, waiting for transfers between devices: 153 us -> 109 us  [on_device(): weights = lax.all_gather(shard, ('dp', 'y'), axis=0)]
    ppermute x0 -> x10, starting transfers between devices: none -> 41.7 us  [shift(): lax.ppermute(array, axis, [(i, (i + by) % size) for i in range(size)])]
    all_gather x1 -> x0, waiting for transfers between devices: 41.2 us -> none  [on_device(): lax.all_gather(pack(tokens, cotangent, routes, combine), GROUP, axis=0, t...]
    reduce_scatter x1 -> x0, waiting for transfers between devices: 38.2 us -> none  [on_device(): mine = lax.psum_scatter(partial, GROUP, scatter_dimension=0)]
    ppermute x0 -> x10, waiting for transfers between devices: none -> 36 us  [shift(): lax.ppermute(array, axis, [(i, (i + by) % size) for i in range(size)])]
    pallas_call x1, Pallas kernels: 41.8 us -> 20.7 us  [experts(): pl.pallas_call(functools.partial(experts_kernel, topk), grid_spec=pltpu.P...]
    reshape x1 -> x0, local copies, waits for them, and re-layouts: 6.4 us -> none  [on_device(): partial = partial.reshape(members, rows, packed.shape[1])]
    pallas_call x0 -> x1, Pallas kernels: none -> 4.63 us  [route(): pl.pallas_call(functools.partial(route_kernel, topk), in_specs=[smem, vme...]
  transfers between devices with their start and end apart: 3 -> 11, of which waited for: 3 -> 10; matrix products, arithmetic and copies ran while one was open for 1% -> 1% of each run, Pallas kernels for 0% -> 2%
where the time goes in v2:
time: 240 us; the launch traced here: 238 us
  waiting for transfers between devices  145 us (60%)
  starting transfers between devices  41.7 us (17%)
  Pallas kernels  25.4 us (11%)
  between operations  14.2 us (6%)
  local copies, waits for them, and re-layouts  8 us (3%)
  other arithmetic  4.26 us (2%)
    all_gather x1, waiting for transfers between devices, on_device(): weights = lax.all_gather(shard, ('dp', 'y'), axis=0)  109 us
    ppermute x10, starting transfers between devices, shift(): lax.ppermute(array, axis, [(i, (i + by) % size) for i in range(size)])  41.7 us
    ppermute x10, waiting for transfers between devices, shift(): lax.ppermute(array, axis, [(i, (i + by) % size) for i in range(size)])  36 us
    pallas_call x1, Pallas kernels, experts(): pl.pallas_call(functools.partial(experts_kernel, topk), grid_spec=pltpu.P...  20.7 us
    unnamed x8, local copies, waits for them, and re-layouts  5.36 us
  transfers between devices with their start and end apart: 11, of which 10 were waited for; matrix products, arithmetic and copies ran while one was open for 1% of the time, Pallas kernels for 2%

profile of v2, /device:TPU:1, one launch (start us, length us, event | category | flops | bytes accessed | tf_op | source)
XLA Modules:
  0.0 238.3 jit_solution(13557778900404120392)
XLA Ops:
  7.2 0.0 all-gather.3.cloned.1.call-start
  7.2 1.0 copy.20
  8.2 1.7 pad_maximum_fusion.2
  9.9 0.0 all-gather.3.cloned.1.call-update
  9.9 0.7 convert_element_type.50
  10.6 0.8 subtract_convert_fusion
  11.4 0.1 copy.19
  11.5 0.1 copy.17
  11.6 0.1 copy.18
  11.8 1.2 concatenate.12
  13.0 3.9 %collective-permute-start.1 = (bf16[128,2176]{1,0:T(8,128)(2,1)S(1)}, bf16[128,2176]{1,0:T(8,128)(2,1)S(1)}, u32[]{:S(2)}, u32[]{:S(2)}) collective-permute-start(bf16[128,2176]{1,0:T(8,128)(2,1)S(1)} %concatenate.12), channel_id=1, source_target_pairs={{0,16},{16,32},{32,48},{48,0},{1,17},{17,33},{33,49},{49,1},{2,18}... | collective-permute-start | bytes 1671176 | tf_op jit(solution)/shard_map/ppermute | solution.py:185
  17.0 3.2 %collective-permute-start = (bf16[128,2176]{1,0:T(8,128)(2,1)S(1)}, bf16[128,2176]{1,0:T(8,128)(2,1)S(1)}, u32[]{:S(2)}, u32[]{:S(2)}) collective-permute-start(bf16[128,2176]{1,0:T(8,128)(2,1)S(1)} %concatenate.12), channel_id=1, source_target_pairs={{0,48},{16,0},{32,16},{48,32},{1,49},{17,1},{33,17},{49,33},{2,50}... | collective-permute-start | bytes 1671176 | tf_op jit(solution)/shard_map/ppermute | solution.py:185
  20.2 4.9 %collective-permute-done.1 = bf16[128,2176]{1,0:T(8,128)(2,1)S(1)} collective-permute-done((bf16[128,2176]{1,0:T(8,128)(2,1)S(1)}, bf16[128,2176]{1,0:T(8,128)(2,1)S(1)}, u32[]{:S(2)}, u32[]{:S(2)}) %collective-permute-start.1) | collective-permute-done | bytes 557088 | tf_op jit(solution)/shard_map/ppermute | solution.py:185
  25.2 6.2 %collective-permute-start.2 = (bf16[64,2176]{1,0:T(8,128)(2,1)S(1)}, bf16[64,2176]{1,0:T(8,128)(2,1)S(1)}, u32[]{:S(2)}, u32[]{:S(2)}) collective-permute-start(bf16[64,2176]{1,0:T(8,128)(2,1)S(1)} %slice.66), channel_id=1, source_target_pairs={{0,16},{16,32},{32,48},{48,0},{1,17},{17,33},{33,49},{49,1},{2,18}... | collective-permute-start | bytes 835592 | tf_op jit(solution)/shard_map/ppermute | solution.py:185
  31.4 0.0 collective-permute-done
  31.4 4.2 %collective-permute-start.3 = (bf16[64,2176]{1,0:T(8,128)(2,1)S(1)}, bf16[64,2176]{1,0:T(8,128)(2,1)S(1)}, u32[]{:S(2)}, u32[]{:S(2)}) collective-permute-start(bf16[64,2176]{1,0:T(8,128)(2,1)S(1)} %slice.67), channel_id=1, source_target_pairs={{0,48},{16,0},{32,16},{48,32},{1,49},{17,1},{33,17},{49,33},{2,50}... | collective-permute-start | bytes 835592 | tf_op jit(solution)/shard_map/ppermute | solution.py:185
  35.6 0.1 constant_dynamic-update-slice_fusion.3
  35.7 2.3 collective-permute-done.2
  38.0 2.0 collective-permute-done.3
  40.0 0.1 constant_dynamic-update-slice_fusion.own_ref
  40.1 5.6 %collective-permute-start.4 = (bf16[512,2176]{1,0:T(8,128)(2,1)S(1)}, bf16[512,2176]{1,0:T(8,128)(2,1)}, u32[]{:S(2)}, u32[]{:S(2)}) collective-permute-start(bf16[512,2176]{1,0:T(8,128)(2,1)S(1)} %constant_dynamic-update-slice_fusion.own_ref), channel_id=1, source_target_pairs={{0,1},{1,0},{2,3},{3,2},{4,5},{5,4},{6,7},{7,6},{8,9},{9,8},{10,11... | collective-permute-start | bytes 6684680 | tf_op jit(solution)/shard_map/ppermute | solution.py:185
  45.7 0.1 pad_add_fusion.first_ref
  45.8 4.0 %collective-permute-done.4.other_ref = bf16[512,2176]{1,0:T(8,128)(2,1)} collective-permute-done((bf16[512,2176]{1,0:T(8,128)(2,1)S(1)}, bf16[512,2176]{1,0:T(8,128)(2,1)}, u32[]{:S(2)}, u32[]{:S(2)}) %collective-permute-start.4) | collective-permute-done | bytes 2228256 | tf_op jit(solution)/shard_map/ppermute | solution.py:185
  49.8 4.6 %shard_map.94 = (bf16[16,8,16,2176]{3,2,1,0:T(8,128)(2,1)S(1)}, bf16[8,256,128]{2,1,0:T(8,128)(2,1)S(1)}, s32[17]{0:T(128)S(1)}) custom-call(s32[2]{0:T(128)S(1)} %pad_add_fusion.first_ref, bf16[512,2176]{1,0:T(8,128)(2,1)S(1)} %constant_dynamic-update-slice_fusion.own_ref, bf16[512,2176]{1,0:T(8,128)(2,1)} %collective-permute-done.4.other_ref), custom_call_target="tpu_custom_call" | custom-call | flops 1140850688 | bytes 18000000 | tf_op jit(solution)/shard_map/pallas_call | solution.py:140
  54.4 0.0 copy-start
  54.4 3.5 %copy-done = bf16[16,8,16,2176]{3,2,1,0:T(8,128)(2,1)} copy-done((bf16[16,8,16,2176]{3,2,1,0:T(8,128)(2,1)}, bf16[16,8,16,2176]{3,2,1,0:T(8,128)(2,1)S(1)}, u32[]{:S(2)}) %copy-start) | copy-done | bytes 8912920
  58.0 108.7 %all-gather.3.cloned.1.call-done = bf16[192,128,384]{2,1,0:T(8,128)(2,1)} async-done(((bf16[3,128,384]{2,1,0:T(8,128)(2,1)}), bf16[192,128,384]{2,1,0:T(8,128)(2,1)}) %all-gather.3.cloned.1.call-update) | async-done | bytes 18874384 | tf_op jit(solution)/shard_map/all_gather | solution.py:216
  166.7 20.7 %shard_map.95 = (bf16[512,2176]{1,0:T(8,128)(2,1)S(1)}, bf16[512,2176]{1,0:T(8,128)(2,1)S(1)}) custom-call(s32[2]{0:T(128)S(1)} %pad_add_fusion.first_ref, s32[17]{0:T(128)S(1)} %get-tuple-element.8.table_ref, bf16[16,8,16,2176]{3,2,1,0:T(8,128)(2,1)} %copy-done, bf16[8,256,128]{2,1,0:T(8,128)(2,1)S(1)} %get-tuple-element.10.pick_ref, ...), custom_call_target="tpu_custom_call" | custom-call | flops 9663676416 | bytes 36000000 | tf_op jit(solution)/shard_map/pallas_call | solution.py:162
  187.4 4.8 %collective-permute-start.5 = (bf16[512,2176]{1,0:T(8,128)(2,1)S(1)}, bf16[512,2176]{1,0:T(8,128)(2,1)S(1)}, u32[]{:S(2)}, u32[]{:S(2)}) collective-permute-start(bf16[512,2176]{1,0:T(8,128)(2,1)S(1)} %get-tuple-element.12), channel_id=1, source_target_pairs={{0,1},{1,0},{2,3},{3,2},{4,5},{5,4},{6,7},{7,6},{8,9},{9,8},{10,11... | collective-permute-start | bytes 6684680 | tf_op jit(solution)/shard_map/ppermute | solution.py:185
  192.2 4.0 %collective-permute-done.5 = bf16[512,2176]{1,0:T(8,128)(2,1)S(1)} collective-permute-done((bf16[512,2176]{1,0:T(8,128)(2,1)S(1)}, bf16[512,2176]{1,0:T(8,128)(2,1)S(1)}, u32[]{:S(2)}, u32[]{:S(2)}) %collective-permute-start.5) | collective-permute-done | bytes 2228256 | tf_op jit(solution)/shard_map/ppermute | solution.py:185
  196.2 0.5 add_convert_fusion
  196.7 0.1 fusion.1
  196.8 1.9 collective-permute-start.6
  198.7 4.6 %collective-permute-start.8 = (bf16[64,2176]{1,0:T(8,128)(2,1)S(1)}, bf16[64,2176]{1,0:T(8,128)(2,1)S(1)}, u32[]{:S(2)}, u32[]{:S(2)}) collective-permute-start(bf16[64,2176]{1,0:T(8,128)(2,1)S(1)} %get-tuple-element.26), channel_id=1, source_target_pairs={{0,48},{16,0},{32,16},{48,32},{1,49},{17,1},{33,17},{49,33},{2,50}... | collective-permute-start | bytes 835592 | tf_op jit(solution)/shard_map/ppermute | solution.py:185
  203.3 4.5 %collective-permute-done.6 = bf16[64,2176]{1,0:T(8,128)(2,1)S(1)} collective-permute-done((bf16[64,2176]{1,0:T(8,128)(2,1)S(1)}, bf16[64,2176]{1,0:T(8,128)(2,1)S(1)}, u32[]{:S(2)}, u32[]{:S(2)}) %collective-permute-start.6) | collective-permute-done | bytes 278560 | tf_op jit(solution)/shard_map/ppermute | solution.py:185
  207.8 0.9 collective-permute-done.8
  208.6 0.1 add_convert_fusion.2
  208.8 5.3 %collective-permute-start.9 = (bf16[128,2176]{1,0:T(8,128)(2,1)S(1)}, bf16[128,2176]{1,0:T(8,128)(2,1)S(1)}, u32[]{:S(2)}, u32[]{:S(2)}) collective-permute-start(bf16[128,2176]{1,0:T(8,128)(2,1)S(1)} %pad_maximum_fusion.1), channel_id=1, source_target_pairs={{0,48},{16,0},{32,16},{48,32},{1,49},{17,1},{33,17},{49,33},{2,50}... | collective-permute-start | bytes 1671176 | tf_op jit(solution)/shard_map/ppermute | solution.py:185
  214.2 1.9 collective-permute-start.7
  216.1 8.4 %collective-permute-done.9 = bf16[128,2176]{1,0:T(8,128)(2,1)S(1)} collective-permute-done((bf16[128,2176]{1,0:T(8,128)(2,1)S(1)}, bf16[128,2176]{1,0:T(8,128)(2,1)S(1)}, u32[]{:S(2)}, u32[]{:S(2)}) %collective-permute-start.9) | collective-permute-done | bytes 557088 | tf_op jit(solution)/shard_map/ppermute | solution.py:185
  224.5 5.1 %collective-permute-done.7 = bf16[128,2176]{1,0:T(8,128)(2,1)S(1)} collective-permute-done((bf16[128,2176]{1,0:T(8,128)(2,1)S(1)}, bf16[128,2176]{1,0:T(8,128)(2,1)S(1)}, u32[]{:S(2)}, u32[]{:S(2)}) %collective-permute-start.7) | collective-permute-done | bytes 557088 | tf_op jit(solution)/shard_map/ppermute | solution.py:185
  229.6 0.2 fusion
  229.8 0.9 fusion.2
  230.7 0.1 slice_add_fusion
  230.8 0.7 copy.21
  (8 shorter events, 0.2 us)
Async XLA Ops:
  7.2 159.5 %all-gather.3.cloned.1.call-start = ((), (), s32[]{:S(2)}) async-start(), calls=%async_computation | async-start | bytes 19169280 | tf_op jit(solution)/shard_map/all_gather | solution.py:216
  13.0 12.1 %collective-permute-start.1 = (bf16[128,2176]{1,0:T(8,128)(2,1)S(1)}, bf16[128,2176]{1,0:T(8,128)(2,1)S(1)}, u32[]{:S(2)}, u32[]{:S(2)}) collective-permute-start(bf16[128,2176]{1,0:T(8,128)(2,1)S(1)} %concatenate.12), channel_id=1, source_target_pairs={{0,16},{16,32},{32,48},{48,0},{1,17},{17,33},{33,49},{49,1},{2,18}... | collective-permute-start | bytes 1671176 | tf_op jit(solution)/shard_map/ppermute | solution.py:185
  17.0 14.4 %collective-permute-start = (bf16[128,2176]{1,0:T(8,128)(2,1)S(1)}, bf16[128,2176]{1,0:T(8,128)(2,1)S(1)}, u32[]{:S(2)}, u32[]{:S(2)}) collective-permute-start(bf16[128,2176]{1,0:T(8,128)(2,1)S(1)} %concatenate.12), channel_id=1, source_target_pairs={{0,48},{16,0},{32,16},{48,32},{1,49},{17,1},{33,17},{49,33},{2,50}... | collective-permute-start | bytes 1671176 | tf_op jit(solution)/shard_map/ppermute | solution.py:185
  25.2 12.8 %collective-permute-start.2 = (bf16[64,2176]{1,0:T(8,128)(2,1)S(1)}, bf16[64,2176]{1,0:T(8,128)(2,1)S(1)}, u32[]{:S(2)}, u32[]{:S(2)}) collective-permute-start(bf16[64,2176]{1,0:T(8,128)(2,1)S(1)} %slice.66), channel_id=1, source_target_pairs={{0,16},{16,32},{32,48},{48,0},{1,17},{17,33},{33,49},{49,1},{2,18}... | collective-permute-start | bytes 835592 | tf_op jit(solution)/shard_map/ppermute | solution.py:185
  31.4 8.6 %collective-permute-start.3 = (bf16[64,2176]{1,0:T(8,128)(2,1)S(1)}, bf16[64,2176]{1,0:T(8,128)(2,1)S(1)}, u32[]{:S(2)}, u32[]{:S(2)}) collective-permute-start(bf16[64,2176]{1,0:T(8,128)(2,1)S(1)} %slice.67), channel_id=1, source_target_pairs={{0,48},{16,0},{32,16},{48,32},{1,49},{17,1},{33,17},{49,33},{2,50}... | collective-permute-start | bytes 835592 | tf_op jit(solution)/shard_map/ppermute | solution.py:185
  40.1 9.7 %collective-permute-start.4 = (bf16[512,2176]{1,0:T(8,128)(2,1)S(1)}, bf16[512,2176]{1,0:T(8,128)(2,1)}, u32[]{:S(2)}, u32[]{:S(2)}) collective-permute-start(bf16[512,2176]{1,0:T(8,128)(2,1)S(1)} %constant_dynamic-update-slice_fusion.own_ref), channel_id=1, source_target_pairs={{0,1},{1,0},{2,3},{3,2},{4,5},{5,4},{6,7},{7,6},{8,9},{9,8},{10,11... | collective-permute-start | bytes 6684680 | tf_op jit(solution)/shard_map/ppermute | solution.py:185
  54.4 3.5 %copy-start = (bf16[16,8,16,2176]{3,2,1,0:T(8,128)(2,1)}, bf16[16,8,16,2176]{3,2,1,0:T(8,128)(2,1)S(1)}, u32[]{:S(2)}) copy-start(bf16[16,8,16,2176]{3,2,1,0:T(8,128)(2,1)S(1)} %get-tuple-element.9.rows_ref) | copy-start | bytes 26738692
  187.4 8.7 %collective-permute-start.5 = (bf16[512,2176]{1,0:T(8,128)(2,1)S(1)}, bf16[512,2176]{1,0:T(8,128)(2,1)S(1)}, u32[]{:S(2)}, u32[]{:S(2)}) collective-permute-start(bf16[512,2176]{1,0:T(8,128)(2,1)S(1)} %get-tuple-element.12), channel_id=1, source_target_pairs={{0,1},{1,0},{2,3},{3,2},{4,5},{5,4},{6,7},{7,6},{8,9},{9,8},{10,11... | collective-permute-start | bytes 6684680 | tf_op jit(solution)/shard_map/ppermute | solution.py:185
  196.8 11.0 %collective-permute-start.6 = (bf16[64,2176]{1,0:T(8,128)(2,1)S(1)}, bf16[64,2176]{1,0:T(8,128)(2,1)S(1)}, u32[]{:S(2)}, u32[]{:S(2)}) collective-permute-start(bf16[64,2176]{1,0:T(8,128)(2,1)S(1)} %get-tuple-element.25), channel_id=1, source_target_pairs={{0,16},{16,32},{32,48},{48,0},{1,17},{17,33},{33,49},{49,1},{2,18}... | collective-permute-start | bytes 835592 | tf_op jit(solution)/shard_map/ppermute | solution.py:185
  198.7 9.9 %collective-permute-start.8 = (bf16[64,2176]{1,0:T(8,128)(2,1)S(1)}, bf16[64,2176]{1,0:T(8,128)(2,1)S(1)}, u32[]{:S(2)}, u32[]{:S(2)}) collective-permute-start(bf16[64,2176]{1,0:T(8,128)(2,1)S(1)} %get-tuple-element.26), channel_id=1, source_target_pairs={{0,48},{16,0},{32,16},{48,32},{1,49},{17,1},{33,17},{49,33},{2,50}... | collective-permute-start | bytes 835592 | tf_op jit(solution)/shard_map/ppermute | solution.py:185
  208.8 15.7 %collective-permute-start.9 = (bf16[128,2176]{1,0:T(8,128)(2,1)S(1)}, bf16[128,2176]{1,0:T(8,128)(2,1)S(1)}, u32[]{:S(2)}, u32[]{:S(2)}) collective-permute-start(bf16[128,2176]{1,0:T(8,128)(2,1)S(1)} %pad_maximum_fusion.1), channel_id=1, source_target_pairs={{0,48},{16,0},{32,16},{48,32},{1,49},{17,1},{33,17},{49,33},{2,50}... | collective-permute-start | bytes 1671176 | tf_op jit(solution)/shard_map/ppermute | solution.py:185
  214.2 15.4 %collective-permute-start.7 = (bf16[128,2176]{1,0:T(8,128)(2,1)S(1)}, bf16[128,2176]{1,0:T(8,128)(2,1)S(1)}, u32[]{:S(2)}, u32[]{:S(2)}) collective-permute-start(bf16[128,2176]{1,0:T(8,128)(2,1)S(1)} %pad_maximum_fusion), channel_id=1, source_target_pairs={{0,16},{16,32},{32,48},{48,0},{1,17},{17,33},{33,49},{49,1},{2,18}... | collective-permute-start | bytes 1671176 | tf_op jit(solution)/shard_map/ppermute | solution.py:185
Sparse Core Ops, SparseCore 0:
  11.0 155.6 all-gather.2

commit v3 on v2

--- a/solution.py
+++ b/solution.py
@@ -85,7 +85,8 @@
     wide = rows_ref.shape[3]
     width = (wide - META) // 2
     count = blocks * SLOTS
-    depth = w_ref.shape[0] * w_ref.shape[3]
+    zs, part = w_ref.shape[0], w_ref.shape[2]
+    hidden_units = w_ref.shape[3] // 3
 
     @pl.when(q >= table_ref[chunks])
     def _():
@@ -95,9 +96,14 @@
     def _():
         name = (first_ref[0] + table_ref[q] * first_ref[1]).astype(F32)
 
-        def weight(which):
-            return w_ref[:, 0, which].reshape(depth, w_ref.shape[4])
-
+        gate_up = w_ref[:, 0, :, : 2 * hidden_units].reshape(zs * part, 2 * hidden_units)
+        down = jnp.concatenate(
+            [
+                jnp.concatenate([w_ref[z, 0, :, at : at + META] for z in range(zs)], axis=1)
+                for at in range(2 * hidden_units, 3 * hidden_units, META)
+            ],
+            axis=0,
+        )
         x = rows_ref[0, :, :, :width].reshape(count, width)
         dy = rows_ref[0, :, :, width : 2 * width].reshape(count, width)
         meta = rows_ref[0, :, :, 2 * width :].astype(F32).reshape(count, META)
@@ -105,16 +111,16 @@
         hit = (meta == name) & (lane < topk)
         both = pltpu.roll(meta, META - topk, 1) + pltpu.roll(meta, META - 2 * topk, 1)
         g = jnp.sum(jnp.where(hit, both, 0.0), axis=1, keepdims=True)
-        gate = nn(x, weight(0))
-        up = nn(x, weight(1))
+        pre = nn(x, gate_up)
+        gate, up = pre[:, :hidden_units], pre[:, hidden_units:]
         sig = jax.nn.sigmoid(gate)
         silu = gate * sig
         hidden = (silu * up).astype(BF)
-        hidden_grad = g * nn(dy, weight(2))
+        hidden_grad = g * nt(dy, down)
         gate_grad = (hidden_grad * up * sig * (1.0 + gate * (1.0 - sig))).astype(BF)
         up_grad = (hidden_grad * silu).astype(BF)
-        eo = nt(hidden, weight(2)).astype(BF).astype(F32)
-        grad = (nt(gate_grad, weight(0)) + nt(up_grad, weight(1))).astype(BF)
+        eo = nn(hidden, down).astype(BF).astype(F32)
+        grad = (nt(jnp.concatenate([gate_grad, up_grad], axis=1), gate_up)).astype(BF)
         cg = jnp.sum(eo * dy.astype(F32), axis=1, keepdims=True)
         cg_high = cg.astype(BF).astype(F32)
         tail = jnp.where(hit, cg_high, 0.0) + pltpu.roll(jnp.where(hit, cg - cg_high, 0.0), topk, 1)
@@ -128,8 +134,8 @@
         half = blocks // 2
         for b in range(blocks):
             ref = own_ref if b < half else other_ref
-            at = (b % half) * size
-            ref[at : at + size] = tn(pick_ref[b], back_ref[:, b].reshape(slots, wide)).astype(BF)
+            at = lax.rem(first_ref[2] + b % half, half) * size
+            ref[pl.ds(pl.multiple_of(at, size), size)] = tn(pick_ref[b], back_ref[:, b].reshape(slots, wide)).astype(BF)
 
 
 def route(first, own, other, local, topk):
@@ -155,7 +161,7 @@
 
 
 def experts(first, table, rows, pick, weights, topk):
-    zs, local, three, part, hidden = weights.shape
+    zs, local, part, hidden = weights.shape
     chunks, blocks, slots, wide = rows.shape
     half = blocks * SIZE // 2
     whole = pl.BlockSpec((half, wide), lambda q, s, t: (0, 0))
@@ -165,9 +171,9 @@
             num_scalar_prefetch=2,
             grid=(chunks,),
             in_specs=[
-                pl.BlockSpec((1, blocks, slots, wide), lambda q, s, t: (q, 0, 0, 0)),
+                pl.BlockSpec((1, blocks, slots, wide), lambda q, s, t: (jnp.minimum(q, t[chunks] - 1), 0, 0, 0)),
                 pl.BlockSpec(pick.shape, lambda q, s, t: (0, 0, 0)),
-                pl.BlockSpec((zs, 1, three, part, hidden), lambda q, s, t: (0, t[q], 0, 0, 0)),
+                pl.BlockSpec((zs, 1, part, hidden), lambda q, s, t: (0, t[q], 0, 0)),
             ],
             out_specs=[whole, whole],
             scratch_shapes=[pltpu.VMEM(rows.shape, BF)],
@@ -175,7 +181,7 @@
         out_shape=[jax.ShapeDtypeStruct((half, wide), BF)] * 2,
         compiler_params=pltpu.CompilerParams(vmem_limit_bytes=48 * 1024 * 1024),
         cost_estimate=pl.CostEstimate(
-            flops=2 * 6 * CHUNKS * SIZE * 1024 * hidden, bytes_accessed=36_000_000, transcendentals=0
+            flops=2 * 2 * CHUNKS * SIZE * 1024 * hidden, bytes_accessed=36_000_000, transcendentals=0
         ),
     )(first, table, rows, pick, weights)
 
@@ -198,27 +204,24 @@
 
 
 def sum_group(mine, other):
-    total = add(mine, shift(other, "core", 1))
-    size = total.shape[0] // 4
-    middle = size // 2
-    part = [total[o * size : (o + 1) * size] for o in range(4)]
-    from_left = shift(part[2][:middle], "x", 1)
-    from_right = shift(part[2][middle:], "x", -1)
-    to_right = jnp.concatenate([add(part[1][:middle], from_left), part[1][middle:]], axis=0)
-    to_left = jnp.concatenate([part[3][:middle], add(part[3][middle:], from_right)], axis=0)
-    return part[0].astype(F32) + shift(to_right, "x", 1).astype(F32) + shift(to_left, "x", -1).astype(F32)
+    size = lax.axis_size("x")
+    total = add(mine, shift(other, "core", 1)).reshape((size, mine.shape[0] // size, mine.shape[1]))
+    parts = lax.all_to_all(total, "x", 0, 0, tiled=True)
+    return jnp.sum(parts.astype(F32), axis=0)
 
 
 def on_device(tokens, cotangent, routes, combine, w_gate, w_up, w_down):
     width = tokens.shape[1]
     topk = routes.shape[1]
-    shard = jnp.stack([w_gate[0], w_up[0], w_down[0].T])
+    down = w_down[0]
+    cuts = [down[at : at + META] for at in range(0, down.shape[0], META)]
+    shard = jnp.concatenate([w_gate[0], w_up[0]] + cuts, axis=1)
     weights = lax.all_gather(shard, ("dp", "y"), axis=0)
     weights = weights.reshape((lax.axis_size("dp"), lax.axis_size("y")) + shard.shape)
     mine, other = gather_group(pack(tokens, cotangent, routes, combine))
     cores = lax.axis_size("core")
     first = lax.axis_index("x") * lax.axis_size("y") * cores + lax.axis_index("core")
-    first = jnp.stack([first, jnp.full_like(first, cores)])
+    first = jnp.stack([first, jnp.full_like(first, cores), lax.axis_index("x")])
     rows, pick, table = route(first, mine, other, weights.shape[1], topk)
     total = sum_group(*experts(first, table, rows, pick, weights, topk))
     tail = total[:, 2 * width :]

time: 240 us -> 235 us (0.979)
  blocking collectives: 0 us -> 30 us
  waiting for transfers between devices: 145 us -> 125 us
  starting transfers between devices: 41.7 us -> 25.1 us
  local copies, waits for them, and re-layouts: 8 us -> 11.8 us
    all_to_all x0 -> x1, blocking collectives: none -> 30 us  [sum_group(): parts = lax.all_to_all(total, 'x', 0, 0, tiled=True)]
    ppermute x10 -> x6, waiting for transfers between devices: 36 us -> 17.5 us  [shift(): lax.ppermute(array, axis, [(i, (i + by) % size) for i in range(size)])]
    ppermute x10 -> x6, starting transfers between devices: 41.7 us -> 25.1 us  [shift(): lax.ppermute(array, axis, [(i, (i + by) % size) for i in range(size)])]
    unnamed x8 -> x13, local copies, waits for them, and re-layouts: 5.36 us -> 8.43 us
  transfers between devices with their start and end apart: 11 -> 7, of which waited for: 10 -> 6; matrix products, arithmetic and copies ran while one was open for 1% -> 1% of each run, Pallas kernels for 2% -> 2%
where the time goes in v3:
time: 235 us; the launch traced here: 234 us
  waiting for transfers between devices  125 us (53%)
  blocking collectives  30 us (13%)
  Pallas kernels  25.3 us (11%)
  starting transfers between devices  25.1 us (11%)
  between operations  14.2 us (6%)
  local copies, waits for them, and re-layouts  11.8 us (5%)
  other arithmetic  2.52 us (1%)
    all_gather x1, waiting for transfers between devices, on_device(): weights = lax.all_gather(shard, ('dp', 'y'), axis=0)  108 us
    all_to_all x1, blocking collectives, sum_group(): parts = lax.all_to_all(total, 'x', 0, 0, tiled=True)  30 us
    ppermute x6, starting transfers between devices, shift(): lax.ppermute(array, axis, [(i, (i + by) % size) for i in range(size)])  25.1 us
    pallas_call x1, Pallas kernels, experts(): pl.pallas_call(functools.partial(experts_kernel, topk), grid_spec=pltpu.P...  20.6 us
    ppermute x6, waiting for transfers between devices, shift(): lax.ppermute(array, axis, [(i, (i + by) % size) for i in range(size)])  17.5 us
    unnamed x13, local copies, waits for them, and re-layouts  8.43 us
  transfers between devices with their start and end apart: 7, of which 6 were waited for; matrix products, arithmetic and copies ran while one was open for 1% of the time, Pallas kernels for 2%

profile of v3, /device:TPU:1, one launch (start us, length us, event | category | flops | bytes accessed | tf_op | source)
XLA Modules:
  0.0 234.1 jit_solution(7573404652335110374)
XLA Ops:
  7.2 0.0 all-gather.3.cloned.1.call-start
  7.2 0.9 bitcast_dynamic-update-slice_fusion.1
  8.1 0.9 bitcast_dynamic-update-slice_fusion
  9.0 0.8 bitcast_dynamic-update-slice_fusion.4
  9.8 0.8 bitcast_dynamic-update-slice_fusion.3
  10.6 0.8 bitcast_dynamic-update-slice_fusion.2
  11.3 0.0 copy-start.1
  11.3 0.7 copy-done.1
  12.1 0.0 all-gather.3.cloned.1.call-update
  12.1 0.7 convert_element_type.26
  12.8 0.8 subtract_convert_fusion
  13.5 0.1 copy.17
  13.7 0.1 copy.15
  13.8 0.1 copy.16
  13.9 1.2 concatenate.9
  15.2 3.9 %collective-permute-start.1 = (bf16[128,2176]{1,0:T(8,128)(2,1)S(1)}, bf16[128,2176]{1,0:T(8,128)(2,1)S(1)}, u32[]{:S(2)}, u32[]{:S(2)}) collective-permute-start(bf16[128,2176]{1,0:T(8,128)(2,1)S(1)} %concatenate.9), channel_id=1, source_target_pairs={{0,16},{16,32},{32,48},{48,0},{1,17},{17,33},{33,49},{49,1},{2,18}... | collective-permute-start | bytes 1671176 | tf_op jit(solution)/shard_map/ppermute | solution.py:191
  19.1 3.2 %collective-permute-start = (bf16[128,2176]{1,0:T(8,128)(2,1)S(1)}, bf16[128,2176]{1,0:T(8,128)(2,1)S(1)}, u32[]{:S(2)}, u32[]{:S(2)}) collective-permute-start(bf16[128,2176]{1,0:T(8,128)(2,1)S(1)} %concatenate.9), channel_id=1, source_target_pairs={{0,48},{16,0},{32,16},{48,32},{1,49},{17,1},{33,17},{49,33},{2,50}... | collective-permute-start | bytes 1671176 | tf_op jit(solution)/shard_map/ppermute | solution.py:191
  22.4 4.9 %collective-permute-done.1 = bf16[128,2176]{1,0:T(8,128)(2,1)S(1)} collective-permute-done((bf16[128,2176]{1,0:T(8,128)(2,1)S(1)}, bf16[128,2176]{1,0:T(8,128)(2,1)S(1)}, u32[]{:S(2)}, u32[]{:S(2)}) %collective-permute-start.1) | collective-permute-done | bytes 557088 | tf_op jit(solution)/shard_map/ppermute | solution.py:191
  27.3 6.2 %collective-permute-start.2 = (bf16[64,2176]{1,0:T(8,128)(2,1)S(1)}, bf16[64,2176]{1,0:T(8,128)(2,1)S(1)}, u32[]{:S(2)}, u32[]{:S(2)}) collective-permute-start(bf16[64,2176]{1,0:T(8,128)(2,1)S(1)} %slice.53), channel_id=1, source_target_pairs={{0,16},{16,32},{32,48},{48,0},{1,17},{17,33},{33,49},{49,1},{2,18}... | collective-permute-start | bytes 835592 | tf_op jit(solution)/shard_map/ppermute | solution.py:191
  33.5 0.0 collective-permute-done
  33.6 4.2 %collective-permute-start.3 = (bf16[64,2176]{1,0:T(8,128)(2,1)S(1)}, bf16[64,2176]{1,0:T(8,128)(2,1)S(1)}, u32[]{:S(2)}, u32[]{:S(2)}) collective-permute-start(bf16[64,2176]{1,0:T(8,128)(2,1)S(1)} %slice.54), channel_id=1, source_target_pairs={{0,48},{16,0},{32,16},{48,32},{1,49},{17,1},{33,17},{49,33},{2,50}... | collective-permute-start | bytes 835592 | tf_op jit(solution)/shard_map/ppermute | solution.py:191
  37.8 0.1 constant_dynamic-update-slice_fusion.3
  37.8 2.3 collective-permute-done.2
  40.1 2.0 collective-permute-done.3
  42.2 0.1 constant_dynamic-update-slice_fusion.own_ref
  42.2 5.6 %collective-permute-start.4 = (bf16[512,2176]{1,0:T(8,128)(2,1)S(1)}, bf16[512,2176]{1,0:T(8,128)(2,1)}, u32[]{:S(2)}, u32[]{:S(2)}) collective-permute-start(bf16[512,2176]{1,0:T(8,128)(2,1)S(1)} %constant_dynamic-update-slice_fusion.own_ref), channel_id=1, source_target_pairs={{0,1},{1,0},{2,3},{3,2},{4,5},{5,4},{6,7},{7,6},{8,9},{9,8},{10,11... | collective-permute-start | bytes 6684680 | tf_op jit(solution)/shard_map/ppermute | solution.py:191
  47.9 0.1 pad_add_fusion.first_ref
  47.9 4.0 %collective-permute-done.4.other_ref = bf16[512,2176]{1,0:T(8,128)(2,1)} collective-permute-done((bf16[512,2176]{1,0:T(8,128)(2,1)S(1)}, bf16[512,2176]{1,0:T(8,128)(2,1)}, u32[]{:S(2)}, u32[]{:S(2)}) %collective-permute-start.4) | collective-permute-done | bytes 2228256 | tf_op jit(solution)/shard_map/ppermute | solution.py:191
  51.9 4.6 %shard_map.94 = (bf16[16,8,16,2176]{3,2,1,0:T(8,128)(2,1)S(1)}, bf16[8,256,128]{2,1,0:T(8,128)(2,1)S(1)}, s32[17]{0:T(128)S(1)}) custom-call(s32[3]{0:T(128)S(1)} %pad_add_fusion.first_ref, bf16[512,2176]{1,0:T(8,128)(2,1)S(1)} %constant_dynamic-update-slice_fusion.own_ref, bf16[512,2176]{1,0:T(8,128)(2,1)} %collective-permute-done.4.other_ref), custom_call_target="tpu_custom_call" | custom-call | flops 1140850688 | bytes 18000000 | tf_op jit(solution)/shard_map/pallas_call | solution.py:146
  56.6 0.0 copy-start
  56.6 3.5 %copy-done = bf16[16,8,16,2176]{3,2,1,0:T(8,128)(2,1)} copy-done((bf16[16,8,16,2176]{3,2,1,0:T(8,128)(2,1)}, bf16[16,8,16,2176]{3,2,1,0:T(8,128)(2,1)S(1)}, u32[]{:S(2)}) %copy-start) | copy-done | bytes 8912920
  60.1 107.8 %all-gather.3.cloned.1.call-done = bf16[8192,1152]{1,0:T(8,128)(2,1)} async-done(((bf16[128,1152]{1,0:T(8,128)(2,1)}), bf16[8192,1152]{1,0:T(8,128)(2,1)}) %all-gather.3.cloned.1.call-update) | async-done | bytes 18874384 | tf_op jit(solution)/shard_map/all_gather | solution.py:219
  167.9 20.6 %shard_map.95 = (bf16[512,2176]{1,0:T(8,128)(2,1)S(1)}, bf16[512,2176]{1,0:T(8,128)(2,1)S(1)}) custom-call(s32[3]{0:T(128)S(1)} %pad_add_fusion.first_ref, s32[17]{0:T(128)S(1)} %get-tuple-element.8.table_ref, bf16[16,8,16,2176]{3,2,1,0:T(8,128)(2,1)} %copy-done, bf16[8,256,128]{2,1,0:T(8,128)(2,1)S(1)} %get-tuple-element.10.pick_ref, ...), custom_call_target="tpu_custom_call" | custom-call | flops 9663676416 | bytes 36000000 | tf_op jit(solution)/shard_map/pallas_call | solution.py:168
  188.6 1.9 collective-permute-start.5
  190.5 4.3 %collective-permute-done.5 = bf16[512,2176]{1,0:T(8,128)(2,1)S(1)} collective-permute-done((bf16[512,2176]{1,0:T(8,128)(2,1)S(1)}, bf16[512,2176]{1,0:T(8,128)(2,1)S(1)}, u32[]{:S(2)}, u32[]{:S(2)}) %collective-permute-start.5) | collective-permute-done | bytes 2228256 | tf_op jit(solution)/shard_map/ppermute | solution.py:191
  194.8 0.5 add_convert_fusion
  195.3 30.0 %all_to_all.5 = bf16[4,128,2176]{2,1,0:T(8,128)(2,1)S(1)} all-to-all(bf16[4,128,2176]{2,1,0:T(8,128)(2,1)S(1)} %bitcast.14), channel_id=1, replica_groups=mesh['dp'=8,'x'=4,'y'=8,'core'=2] {'x'}, dimensions={0} | all-to-all | bytes 4456448 | tf_op jit(solution)/shard_map/all_to_all | solution.py:209
  225.3 0.3 convert_reduce_fusion
  225.6 0.1 slice_add_fusion
  225.7 0.1 convert.4
  225.8 0.7 copy.18
  226.4 0.9 fusion
  (6 shorter events, 0.1 us)
Async XLA Ops:
  7.2 160.7 %all-gather.3.cloned.1.call-start = ((), (), s32[]{:S(2)}) async-start(), calls=%async_computation.1 | async-start | bytes 19169280 | tf_op jit(solution)/shard_map/all_gather | solution.py:219
  11.3 0.7 copy-start.1
  15.2 12.1 %collective-permute-start.1 = (bf16[128,2176]{1,0:T(8,128)(2,1)S(1)}, bf16[128,2176]{1,0:T(8,128)(2,1)S(1)}, u32[]{:S(2)}, u32[]{:S(2)}) collective-permute-start(bf16[128,2176]{1,0:T(8,128)(2,1)S(1)} %concatenate.9), channel_id=1, source_target_pairs={{0,16},{16,32},{32,48},{48,0},{1,17},{17,33},{33,49},{49,1},{2,18}... | collective-permute-start | bytes 1671176 | tf_op jit(solution)/shard_map/ppermute | solution.py:191
  19.1 14.4 %collective-permute-start = (bf16[128,2176]{1,0:T(8,128)(2,1)S(1)}, bf16[128,2176]{1,0:T(8,128)(2,1)S(1)}, u32[]{:S(2)}, u32[]{:S(2)}) collective-permute-start(bf16[128,2176]{1,0:T(8,128)(2,1)S(1)} %concatenate.9), channel_id=1, source_target_pairs={{0,48},{16,0},{32,16},{48,32},{1,49},{17,1},{33,17},{49,33},{2,50}... | collective-permute-start | bytes 1671176 | tf_op jit(solution)/shard_map/ppermute | solution.py:191
  27.3 12.8 %collective-permute-start.2 = (bf16[64,2176]{1,0:T(8,128)(2,1)S(1)}, bf16[64,2176]{1,0:T(8,128)(2,1)S(1)}, u32[]{:S(2)}, u32[]{:S(2)}) collective-permute-start(bf16[64,2176]{1,0:T(8,128)(2,1)S(1)} %slice.53), channel_id=1, source_target_pairs={{0,16},{16,32},{32,48},{48,0},{1,17},{17,33},{33,49},{49,1},{2,18}... | collective-permute-start | bytes 835592 | tf_op jit(solution)/shard_map/ppermute | solution.py:191
  33.6 8.6 %collective-permute-start.3 = (bf16[64,2176]{1,0:T(8,128)(2,1)S(1)}, bf16[64,2176]{1,0:T(8,128)(2,1)S(1)}, u32[]{:S(2)}, u32[]{:S(2)}) collective-permute-start(bf16[64,2176]{1,0:T(8,128)(2,1)S(1)} %slice.54), channel_id=1, source_target_pairs={{0,48},{16,0},{32,16},{48,32},{1,49},{17,1},{33,17},{49,33},{2,50}... | collective-permute-start | bytes 835592 | tf_op jit(solution)/shard_map/ppermute | solution.py:191
  42.2 9.7 %collective-permute-start.4 = (bf16[512,2176]{1,0:T(8,128)(2,1)S(1)}, bf16[512,2176]{1,0:T(8,128)(2,1)}, u32[]{:S(2)}, u32[]{:S(2)}) collective-permute-start(bf16[512,2176]{1,0:T(8,128)(2,1)S(1)} %constant_dynamic-update-slice_fusion.own_ref), channel_id=1, source_target_pairs={{0,1},{1,0},{2,3},{3,2},{4,5},{5,4},{6,7},{7,6},{8,9},{9,8},{10,11... | collective-permute-start | bytes 6684680 | tf_op jit(solution)/shard_map/ppermute | solution.py:191
  56.6 3.6 %copy-start = (bf16[16,8,16,2176]{3,2,1,0:T(8,128)(2,1)}, bf16[16,8,16,2176]{3,2,1,0:T(8,128)(2,1)S(1)}, u32[]{:S(2)}) copy-start(bf16[16,8,16,2176]{3,2,1,0:T(8,128)(2,1)S(1)} %get-tuple-element.9.rows_ref) | copy-start | bytes 26738692
  188.6 6.2 %collective-permute-start.5 = (bf16[512,2176]{1,0:T(8,128)(2,1)S(1)}, bf16[512,2176]{1,0:T(8,128)(2,1)S(1)}, u32[]{:S(2)}, u32[]{:S(2)}) collective-permute-start(bf16[512,2176]{1,0:T(8,128)(2,1)S(1)} %get-tuple-element.12), channel_id=1, source_target_pairs={{0,1},{1,0},{2,3},{3,2},{4,5},{5,4},{6,7},{7,6},{8,9},{9,8},{10,11... | collective-permute-start | bytes 6684680 | tf_op jit(solution)/shard_map/ppermute | solution.py:191
Sparse Core Ops, SparseCore 0:
  12.2 155.6 all-gather.2

commit v4 on v3

--- a/solution.py
+++ b/solution.py
@@ -9,7 +9,7 @@
 
 SIZE = 128
 SLOTS = 16
-CHUNKS = 16
+CHUNKS = 14
 META = 128
 BF, F32 = jnp.bfloat16, jnp.float32
 
@@ -210,12 +210,28 @@
     return jnp.sum(parts.astype(F32), axis=0)
 
 
+def shard_kernel(gate_ref, up_ref, down_ref, out_ref):
+    units, lanes = down_ref.shape[1:]
+    out_ref[:, :units] = gate_ref[0]
+    out_ref[:, units : 2 * units] = up_ref[0]
+    for at in range(0, units, lanes):
+        out_ref[:, 2 * units + at : 2 * units + at + lanes] = down_ref[0, at : at + lanes]
+
+
+def pack_shard(w_gate, w_up, w_down):
+    part, units = w_gate.shape[1:]
+    return pl.pallas_call(
+        shard_kernel,
+        in_specs=[pl.BlockSpec(memory_space=pltpu.VMEM)] * 3,
+        out_specs=pl.BlockSpec(memory_space=pltpu.VMEM),
+        out_shape=jax.ShapeDtypeStruct((part, 3 * units), BF),
+    )(w_gate, w_up, w_down)
+
+
 def on_device(tokens, cotangent, routes, combine, w_gate, w_up, w_down):
     width = tokens.shape[1]
     topk = routes.shape[1]
-    down = w_down[0]
-    cuts = [down[at : at + META] for at in range(0, down.shape[0], META)]
-    shard = jnp.concatenate([w_gate[0], w_up[0]] + cuts, axis=1)
+    shard = pack_shard(w_gate, w_up, w_down)
     weights = lax.all_gather(shard, ("dp", "y"), axis=0)
     weights = weights.reshape((lax.axis_size("dp"), lax.axis_size("y")) + shard.shape)
     mine, other = gather_group(pack(tokens, cotangent, routes, combine))

time: 235 us -> 237 us (level); the launches traced: 234 us -> 234 us
  local copies, waits for them, and re-layouts: 11.8 us -> 6.51 us
  blocking collectives: 30 us -> 34.3 us
  waiting for transfers between devices: 125 us -> 128 us
  Pallas kernels: 25.3 us -> 22.8 us
    unnamed x13 -> x7, local copies, waits for them, and re-layouts: 8.43 us -> 3.96 us
    all_to_all x1, blocking collectives: 30 us -> 34.3 us  [sum_group(): parts = lax.all_to_all(total, 'x', 0, 0, tiled=True)]
    pallas_call x1, Pallas kernels: 20.6 us -> 16.7 us  [experts(): pl.pallas_call(functools.partial(experts_kernel, topk), grid_spec=pltpu.P...]
    all_gather x1, waiting for transfers between devices: 108 us -> 110 us  [on_device(): weights = lax.all_gather(shard, ('dp', 'y'), axis=0)]
where the time goes in v4:
time: 237 us; the launch traced here: 234 us
  waiting for transfers between devices  128 us (54%)
  blocking collectives  34.3 us (14%)
  starting transfers between devices  25.8 us (11%)
  Pallas kernels  22.8 us (10%)
  between operations  14.2 us (6%)
  local copies, waits for them, and re-layouts  6.51 us (3%)
  other arithmetic  2.52 us (1%)
    all_gather x1, waiting for transfers between devices, on_device(): weights = lax.all_gather(shard, ('dp', 'y'), axis=0)  110 us
    all_to_all x1, blocking collectives, sum_group(): parts = lax.all_to_all(total, 'x', 0, 0, tiled=True)  34.3 us
    ppermute x6, starting transfers between devices, shift(): lax.ppermute(array, axis, [(i, (i + by) % size) for i in range(size)])  25.7 us
    ppermute x6, waiting for transfers between devices, shift(): lax.ppermute(array, axis, [(i, (i + by) % size) for i in range(size)])  17.2 us
    pallas_call x1, Pallas kernels, experts(): pl.pallas_call(functools.partial(experts_kernel, topk), grid_spec=pltpu.P...  16.7 us
  transfers between devices with their start and end apart: 7, of which 6 were waited for; matrix products, arithmetic and copies ran while one was open for 1% of the time, Pallas kernels for 2%

profile of v4, /device:TPU:1, one launch (start us, length us, event | category | flops | bytes accessed | tf_op | source)
XLA Modules:
  0.0 233.7 jit_solution(18150869582024635703)
XLA Ops:
  7.2 0.0 all-gather.3.cloned.1.call-start
  7.2 1.7 shard_map.95
  8.9 0.0 all-gather.3.cloned.1.call-update
  9.0 0.7 convert_element_type.26
  9.7 0.8 subtract_convert_fusion
  10.4 0.1 copy.17
  10.5 0.1 copy.15
  10.7 0.1 copy.16
  10.8 1.2 concatenate.6
  12.0 3.9 %collective-permute-start.1 = (bf16[128,2176]{1,0:T(8,128)(2,1)S(1)}, bf16[128,2176]{1,0:T(8,128)(2,1)S(1)}, u32[]{:S(2)}, u32[]{:S(2)}) collective-permute-start(bf16[128,2176]{1,0:T(8,128)(2,1)S(1)} %concatenate.6), channel_id=1, source_target_pairs={{0,16},{16,32},{32,48},{48,0},{1,17},{17,33},{33,49},{49,1},{2,18}... | collective-permute-start | bytes 1671176 | tf_op jit(solution)/shard_map/ppermute | solution.py:191
  16.0 3.2 %collective-permute-start = (bf16[128,2176]{1,0:T(8,128)(2,1)S(1)}, bf16[128,2176]{1,0:T(8,128)(2,1)S(1)}, u32[]{:S(2)}, u32[]{:S(2)}) collective-permute-start(bf16[128,2176]{1,0:T(8,128)(2,1)S(1)} %concatenate.6), channel_id=1, source_target_pairs={{0,48},{16,0},{32,16},{48,32},{1,49},{17,1},{33,17},{49,33},{2,50}... | collective-permute-start | bytes 1671176 | tf_op jit(solution)/shard_map/ppermute | solution.py:191
  19.2 4.9 %collective-permute-done.1 = bf16[128,2176]{1,0:T(8,128)(2,1)S(1)} collective-permute-done((bf16[128,2176]{1,0:T(8,128)(2,1)S(1)}, bf16[128,2176]{1,0:T(8,128)(2,1)S(1)}, u32[]{:S(2)}, u32[]{:S(2)}) %collective-permute-start.1) | collective-permute-done | bytes 557088 | tf_op jit(solution)/shard_map/ppermute | solution.py:191
  24.2 6.2 %collective-permute-start.2 = (bf16[64,2176]{1,0:T(8,128)(2,1)S(1)}, bf16[64,2176]{1,0:T(8,128)(2,1)S(1)}, u32[]{:S(2)}, u32[]{:S(2)}) collective-permute-start(bf16[64,2176]{1,0:T(8,128)(2,1)S(1)} %slice.29), channel_id=1, source_target_pairs={{0,16},{16,32},{32,48},{48,0},{1,17},{17,33},{33,49},{49,1},{2,18}... | collective-permute-start | bytes 835592 | tf_op jit(solution)/shard_map/ppermute | solution.py:191
  30.4 0.0 collective-permute-done
  30.5 4.2 %collective-permute-start.3 = (bf16[64,2176]{1,0:T(8,128)(2,1)S(1)}, bf16[64,2176]{1,0:T(8,128)(2,1)S(1)}, u32[]{:S(2)}, u32[]{:S(2)}) collective-permute-start(bf16[64,2176]{1,0:T(8,128)(2,1)S(1)} %slice.30), channel_id=1, source_target_pairs={{0,48},{16,0},{32,16},{48,32},{1,49},{17,1},{33,17},{49,33},{2,50}... | collective-permute-start | bytes 835592 | tf_op jit(solution)/shard_map/ppermute | solution.py:191
  34.6 0.1 constant_dynamic-update-slice_fusion.3
  34.7 2.2 collective-permute-done.2
  37.0 2.0 collective-permute-done.3
  39.0 0.1 constant_dynamic-update-slice_fusion.own_ref
  39.1 5.6 %collective-permute-start.4 = (bf16[512,2176]{1,0:T(8,128)(2,1)S(1)}, bf16[512,2176]{1,0:T(8,128)(2,1)}, u32[]{:S(2)}, u32[]{:S(2)}) collective-permute-start(bf16[512,2176]{1,0:T(8,128)(2,1)S(1)} %constant_dynamic-update-slice_fusion.own_ref), channel_id=1, source_target_pairs={{0,1},{1,0},{2,3},{3,2},{4,5},{5,4},{6,7},{7,6},{8,9},{9,8},{10,11... | collective-permute-start | bytes 6684680 | tf_op jit(solution)/shard_map/ppermute | solution.py:191
  44.7 0.1 pad_add_fusion.first_ref
  44.8 4.0 %collective-permute-done.4.other_ref = bf16[512,2176]{1,0:T(8,128)(2,1)} collective-permute-done((bf16[512,2176]{1,0:T(8,128)(2,1)S(1)}, bf16[512,2176]{1,0:T(8,128)(2,1)}, u32[]{:S(2)}, u32[]{:S(2)}) %collective-permute-start.4) | collective-permute-done | bytes 2228256 | tf_op jit(solution)/shard_map/ppermute | solution.py:191
  48.8 4.4 %shard_map.94 = (bf16[14,8,16,2176]{3,2,1,0:T(8,128)(2,1)S(1)}, bf16[8,224,128]{2,1,0:T(8,128)(2,1)S(1)}, s32[15]{0:T(128)S(1)}) custom-call(s32[3]{0:T(128)S(1)} %pad_add_fusion.first_ref, bf16[512,2176]{1,0:T(8,128)(2,1)S(1)} %constant_dynamic-update-slice_fusion.own_ref, bf16[512,2176]{1,0:T(8,128)(2,1)} %collective-permute-done.4.other_ref), custom_call_target="tpu_custom_call" | custom-call | flops 998244352 | bytes 18000000 | tf_op jit(solution)/shard_map/pallas_call | solution.py:146
  53.2 0.0 copy-start
  53.2 3.1 %copy-done = bf16[14,8,16,2176]{3,2,1,0:T(8,128)(2,1)} copy-done((bf16[14,8,16,2176]{3,2,1,0:T(8,128)(2,1)}, bf16[14,8,16,2176]{3,2,1,0:T(8,128)(2,1)S(1)}, u32[]{:S(2)}) %copy-start) | copy-done | bytes 7798808
  56.3 110.4 %all-gather.3.cloned.1.call-done = bf16[8192,1152]{1,0:T(8,128)(2,1)} async-done(((bf16[128,1152]{1,0:T(8,128)(2,1)}), bf16[8192,1152]{1,0:T(8,128)(2,1)}) %all-gather.3.cloned.1.call-update) | async-done | bytes 18874384 | tf_op jit(solution)/shard_map/all_gather | solution.py:235
  166.7 16.7 %shard_map.96 = (bf16[512,2176]{1,0:T(8,128)(2,1)S(1)}, bf16[512,2176]{1,0:T(8,128)(2,1)S(1)}) custom-call(s32[3]{0:T(128)S(1)} %pad_add_fusion.first_ref, s32[15]{0:T(128)S(1)} %get-tuple-element.8.table_ref, bf16[14,8,16,2176]{3,2,1,0:T(8,128)(2,1)} %copy-done, bf16[8,224,128]{2,1,0:T(8,128)(2,1)S(1)} %get-tuple-element.10.pick_ref, ...), custom_call_target="tpu_custom_call" | custom-call | flops 8455716864 | bytes 36000000 | tf_op jit(solution)/shard_map/pallas_call | solution.py:168
  183.5 2.6 %collective-permute-start.5 = (bf16[512,2176]{1,0:T(8,128)(2,1)S(1)}, bf16[512,2176]{1,0:T(8,128)(2,1)S(1)}, u32[]{:S(2)}, u32[]{:S(2)}) collective-permute-start(bf16[512,2176]{1,0:T(8,128)(2,1)S(1)} %get-tuple-element.12), channel_id=1, source_target_pairs={{0,1},{1,0},{2,3},{3,2},{4,5},{5,4},{6,7},{7,6},{8,9},{9,8},{10,11... | collective-permute-start | bytes 6684680 | tf_op jit(solution)/shard_map/ppermute | solution.py:191
  186.0 4.0 %collective-permute-done.5 = bf16[512,2176]{1,0:T(8,128)(2,1)S(1)} collective-permute-done((bf16[512,2176]{1,0:T(8,128)(2,1)S(1)}, bf16[512,2176]{1,0:T(8,128)(2,1)S(1)}, u32[]{:S(2)}, u32[]{:S(2)}) %collective-permute-start.5) | collective-permute-done | bytes 2228256 | tf_op jit(solution)/shard_map/ppermute | solution.py:191
  190.0 0.5 add_convert_fusion
  190.5 34.3 %all_to_all.5 = bf16[4,128,2176]{2,1,0:T(8,128)(2,1)S(1)} all-to-all(bf16[4,128,2176]{2,1,0:T(8,128)(2,1)S(1)} %bitcast.4), channel_id=1, replica_groups=mesh['dp'=8,'x'=4,'y'=8,'core'=2] {'x'}, dimensions={0} | all-to-all | bytes 4456448 | tf_op jit(solution)/shard_map/all_to_all | solution.py:209
  224.9 0.3 convert_reduce_fusion
  225.2 0.1 slice_add_fusion
  225.3 0.1 convert.4
  225.3 0.7 copy.18
  226.0 0.9 fusion
  (6 shorter events, 0.1 us)
Async XLA Ops:
  7.2 159.5 %all-gather.3.cloned.1.call-start = ((), (), s32[]{:S(2)}) async-start(), calls=%async_computation.1 | async-start | bytes 19169280 | tf_op jit(solution)/shard_map/all_gather | solution.py:235
  12.0 12.1 %collective-permute-start.1 = (bf16[128,2176]{1,0:T(8,128)(2,1)S(1)}, bf16[128,2176]{1,0:T(8,128)(2,1)S(1)}, u32[]{:S(2)}, u32[]{:S(2)}) collective-permute-start(bf16[128,2176]{1,0:T(8,128)(2,1)S(1)} %concatenate.6), channel_id=1, source_target_pairs={{0,16},{16,32},{32,48},{48,0},{1,17},{17,33},{33,49},{49,1},{2,18}... | collective-permute-start | bytes 1671176 | tf_op jit(solution)/shard_map/ppermute | solution.py:191
  16.0 14.4 %collective-permute-start = (bf16[128,2176]{1,0:T(8,128)(2,1)S(1)}, bf16[128,2176]{1,0:T(8,128)(2,1)S(1)}, u32[]{:S(2)}, u32[]{:S(2)}) collective-permute-start(bf16[128,2176]{1,0:T(8,128)(2,1)S(1)} %concatenate.6), channel_id=1, source_target_pairs={{0,48},{16,0},{32,16},{48,32},{1,49},{17,1},{33,17},{49,33},{2,50}... | collective-permute-start | bytes 1671176 | tf_op jit(solution)/shard_map/ppermute | solution.py:191
  24.2 12.8 %collective-permute-start.2 = (bf16[64,2176]{1,0:T(8,128)(2,1)S(1)}, bf16[64,2176]{1,0:T(8,128)(2,1)S(1)}, u32[]{:S(2)}, u32[]{:S(2)}) collective-permute-start(bf16[64,2176]{1,0:T(8,128)(2,1)S(1)} %slice.29), channel_id=1, source_target_pairs={{0,16},{16,32},{32,48},{48,0},{1,17},{17,33},{33,49},{49,1},{2,18}... | collective-permute-start | bytes 835592 | tf_op jit(solution)/shard_map/ppermute | solution.py:191
  30.5 8.6 %collective-permute-start.3 = (bf16[64,2176]{1,0:T(8,128)(2,1)S(1)}, bf16[64,2176]{1,0:T(8,128)(2,1)S(1)}, u32[]{:S(2)}, u32[]{:S(2)}) collective-permute-start(bf16[64,2176]{1,0:T(8,128)(2,1)S(1)} %slice.30), channel_id=1, source_target_pairs={{0,48},{16,0},{32,16},{48,32},{1,49},{17,1},{33,17},{49,33},{2,50}... | collective-permute-start | bytes 835592 | tf_op jit(solution)/shard_map/ppermute | solution.py:191
  39.1 9.7 %collective-permute-start.4 = (bf16[512,2176]{1,0:T(8,128)(2,1)S(1)}, bf16[512,2176]{1,0:T(8,128)(2,1)}, u32[]{:S(2)}, u32[]{:S(2)}) collective-permute-start(bf16[512,2176]{1,0:T(8,128)(2,1)S(1)} %constant_dynamic-update-slice_fusion.own_ref), channel_id=1, source_target_pairs={{0,1},{1,0},{2,3},{3,2},{4,5},{5,4},{6,7},{7,6},{8,9},{9,8},{10,11... | collective-permute-start | bytes 6684680 | tf_op jit(solution)/shard_map/ppermute | solution.py:191
  53.2 3.2 %copy-start = (bf16[14,8,16,2176]{3,2,1,0:T(8,128)(2,1)}, bf16[14,8,16,2176]{3,2,1,0:T(8,128)(2,1)S(1)}, u32[]{:S(2)}) copy-start(bf16[14,8,16,2176]{3,2,1,0:T(8,128)(2,1)S(1)} %get-tuple-element.9.rows_ref) | copy-start | bytes 23396356
  183.5 6.5 %collective-permute-start.5 = (bf16[512,2176]{1,0:T(8,128)(2,1)S(1)}, bf16[512,2176]{1,0:T(8,128)(2,1)S(1)}, u32[]{:S(2)}, u32[]{:S(2)}) collective-permute-start(bf16[512,2176]{1,0:T(8,128)(2,1)S(1)} %get-tuple-element.12), channel_id=1, source_target_pairs={{0,1},{1,0},{2,3},{3,2},{4,5},{5,4},{6,7},{7,6},{8,9},{9,8},{10,11... | collective-permute-start | bytes 6684680 | tf_op jit(solution)/shard_map/ppermute | solution.py:191
Sparse Core Ops, SparseCore 0:
  11.0 155.6 all-gather.2

commit v5 on v4

--- a/solution.py
+++ b/solution.py
@@ -59,13 +59,22 @@
     for j in range(local):
         count = jnp.max(rank_ref[:, j]).astype(jnp.int32) + 1
         bases.append(bases[j] + (count + SLOTS - 1) // SLOTS)
-    chunks = table_ref.shape[0] - 1
+    chunks = pick_ref.shape[1] // SLOTS
+    ahead = jnp.int32(0)
     for q in range(chunks):
-        at = jnp.int32(0)
-        for j in range(local - 1):
-            at += (bases[j + 1] <= q).astype(jnp.int32)
+        at, start, end = jnp.int32(0), bases[0], bases[1]
+        for j in range(1, local):
+            past = bases[j] <= q
+            at += past.astype(jnp.int32)
+            start = jnp.where(past, bases[j], start)
+            end = jnp.where(past, bases[j + 1], end)
+        odd = lax.rem(q - start, 2)
+        pair = (odd == 0) & (end - q >= 2)
+        ahead = jnp.where(pair, jnp.int32(min(q + 1, chunks - 1)), ahead)
         table_ref[q] = at
-    table_ref[chunks] = bases[local]
+        table_ref[chunks + 1 + q] = jnp.where(pair, 2, 1 - odd)
+        table_ref[2 * chunks + 1 + q] = ahead
+    table_ref[chunks] = jnp.minimum(bases[local], chunks)
     slot = lax.broadcasted_iota(jnp.int32, (slots, size), 0)
     for b in range(blocks):
         pick = jnp.zeros((slots, size), F32)
@@ -78,13 +87,12 @@
         rows_ref[:, b] = nn(pick, block(b)).astype(BF).reshape(chunks, SLOTS, wide)
 
 
-def experts_kernel(topk, first_ref, table_ref, rows_ref, pick_ref, w_ref, own_ref, other_ref, back_ref):
+def experts_kernel(topk, first_ref, table_ref, rows_ref, next_ref, pick_ref, w_ref, own_ref, other_ref, back_ref):
     q = pl.program_id(0)
     chunks = pl.num_programs(0)
     blocks, slots, size = pick_ref.shape
     wide = rows_ref.shape[3]
     width = (wide - META) // 2
-    count = blocks * SLOTS
     zs, part = w_ref.shape[0], w_ref.shape[2]
     hidden_units = w_ref.shape[3] // 3
 
@@ -92,8 +100,12 @@
     def _():
         back_ref[q] = jnp.zeros(back_ref.shape[1:], BF)
 
-    @pl.when(q < table_ref[chunks])
-    def _():
+    def compute(*refs):
+        count = len(refs) * blocks * SLOTS
+
+        def lanes(at, size):
+            return jnp.concatenate([ref[0, :, :, at : at + size] for ref in refs], axis=0).reshape(count, size)
+
         name = (first_ref[0] + table_ref[q] * first_ref[1]).astype(F32)
 
         gate_up = w_ref[:, 0, :, : 2 * hidden_units].reshape(zs * part, 2 * hidden_units)
@@ -104,9 +116,9 @@
             ],
             axis=0,
         )
-        x = rows_ref[0, :, :, :width].reshape(count, width)
-        dy = rows_ref[0, :, :, width : 2 * width].reshape(count, width)
-        meta = rows_ref[0, :, :, 2 * width :].astype(F32).reshape(count, META)
+        x = lanes(0, width)
+        dy = lanes(width, width)
+        meta = lanes(2 * width, META).astype(F32)
         lane = lax.broadcasted_iota(jnp.int32, meta.shape, 1)
         hit = (meta == name) & (lane < topk)
         both = pltpu.roll(meta, META - topk, 1) + pltpu.roll(meta, META - 2 * topk, 1)
@@ -124,10 +136,24 @@
         cg = jnp.sum(eo * dy.astype(F32), axis=1, keepdims=True)
         cg_high = cg.astype(BF).astype(F32)
         tail = jnp.where(hit, cg_high, 0.0) + pltpu.roll(jnp.where(hit, cg - cg_high, 0.0), topk, 1)
-        cut = (blocks, SLOTS)
-        back_ref[q, :, :, :width] = (g * eo).astype(BF).reshape(cut + (width,))
-        back_ref[q, :, :, width : 2 * width] = grad.reshape(cut + (width,))
-        back_ref[q, :, :, 2 * width :] = tail.astype(BF).reshape(cut + (META,))
+        cut = (len(refs), blocks, SLOTS)
+        mixed = (g * eo).astype(BF).reshape(cut + (width,))
+        grad = grad.reshape(cut + (width,))
+        tail = tail.astype(BF).reshape(cut + (META,))
+        for i in range(len(refs)):
+            back_ref[q + i, :, :, :width] = mixed[i]
+            back_ref[q + i, :, :, width : 2 * width] = grad[i]
+            back_ref[q + i, :, :, 2 * width :] = tail[i]
+
+    kind = table_ref[chunks + 1 + q]
+
+    @pl.when((q < table_ref[chunks]) & (kind == 1))
+    def _():
+        compute(rows_ref)
+
+    @pl.when((q < table_ref[chunks] - 1) & (kind == 2))
+    def _():
+        compute(rows_ref, next_ref)
 
     @pl.when(q == chunks - 1)
     def _():
@@ -150,7 +176,7 @@
         out_shape=[
             jax.ShapeDtypeStruct((CHUNKS, blocks, SLOTS, wide), BF),
             jax.ShapeDtypeStruct((blocks, CHUNKS * SLOTS, SIZE), BF),
-            jax.ShapeDtypeStruct((CHUNKS + 1,), jnp.int32),
+            jax.ShapeDtypeStruct((3 * CHUNKS + 1,), jnp.int32),
         ],
         scratch_shapes=[pltpu.VMEM((blocks, local, SIZE), F32)],
         compiler_params=pltpu.CompilerParams(vmem_limit_bytes=40 * 1024 * 1024),
@@ -172,6 +198,7 @@
             grid=(chunks,),
             in_specs=[
                 pl.BlockSpec((1, blocks, slots, wide), lambda q, s, t: (jnp.minimum(q, t[chunks] - 1), 0, 0, 0)),
+                pl.BlockSpec((1, blocks, slots, wide), lambda q, s, t: (t[2 * chunks + 1 + q], 0, 0, 0)),
                 pl.BlockSpec(pick.shape, lambda q, s, t: (0, 0, 0)),
                 pl.BlockSpec((zs, 1, part, hidden), lambda q, s, t: (0, t[q], 0, 0)),
             ],
@@ -183,7 +210,7 @@
         cost_estimate=pl.CostEstimate(
             flops=2 * 2 * CHUNKS * SIZE * 1024 * hidden, bytes_accessed=36_000_000, transcendentals=0
         ),
-    )(first, table, rows, pick, weights)
+    )(first, table, rows, rows, pick, weights)
 
 
 def shift(array, axis, by):

time: 237 us -> 235 us (level); the launches traced: 234 us -> 235 us
  no operation moved by 1% of the time
where the time goes in v5:
time: 235 us
  waiting for transfers between devices  127 us (54%)
  blocking collectives  34.8 us (15%)
  starting transfers between devices  25.8 us (11%)
  Pallas kernels  24 us (10%)
  between operations  14.2 us (6%)
  local copies, waits for them, and re-layouts  6.51 us (3%)
  other arithmetic  2.52 us (1%)
    all_gather x1, waiting for transfers between devices, on_device(): weights = lax.all_gather(shard, ('dp', 'y'), axis=0)  110 us
    all_to_all x1, blocking collectives, sum_group(): parts = lax.all_to_all(total, 'x', 0, 0, tiled=True)  34.8 us
    ppermute x6, starting transfers between devices, shift(): lax.ppermute(array, axis, [(i, (i + by) % size) for i in range(size)])  25.7 us
    pallas_call x1, Pallas kernels, experts(): pl.pallas_call(functools.partial(experts_kernel, topk), grid_spec=pltpu.P...  17.3 us
    ppermute x6, waiting for transfers between devices, shift(): lax.ppermute(array, axis, [(i, (i + by) % size) for i in range(size)])  17.2 us
    pallas_call x1, Pallas kernels, route(): pl.pallas_call(functools.partial(route_kernel, topk), in_specs=[smem, vme...  5 us
  transfers between devices with their start and end apart: 7, of which 6 were waited for; matrix products, arithmetic and copies ran while one was open for 1% of the time, Pallas kernels for 2%

profile of v5, /device:TPU:1, one launch (start us, length us, event | category | flops | bytes accessed | tf_op | source)
XLA Modules:
  0.0 234.7 jit_solution(3575718445022194889)
XLA Ops:
  7.2 0.0 all-gather.3.cloned.1.call-start
  7.2 1.7 shard_map.95
  8.9 0.0 all-gather.3.cloned.1.call-update
  9.0 0.7 convert_element_type.26
  9.7 0.8 subtract_convert_fusion
  10.4 0.1 copy.17
  10.5 0.1 copy.15
  10.7 0.1 copy.16
  10.8 1.2 concatenate.6
  12.0 3.9 %collective-permute-start.1 = (bf16[128,2176]{1,0:T(8,128)(2,1)S(1)}, bf16[128,2176]{1,0:T(8,128)(2,1)S(1)}, u32[]{:S(2)}, u32[]{:S(2)}) collective-permute-start(bf16[128,2176]{1,0:T(8,128)(2,1)S(1)} %concatenate.6), channel_id=1, source_target_pairs={{0,16},{16,32},{32,48},{48,0},{1,17},{17,33},{33,49},{49,1},{2,18}... | collective-permute-start | bytes 1671176 | tf_op jit(solution)/shard_map/ppermute | solution.py:218
  16.0 3.2 %collective-permute-start = (bf16[128,2176]{1,0:T(8,128)(2,1)S(1)}, bf16[128,2176]{1,0:T(8,128)(2,1)S(1)}, u32[]{:S(2)}, u32[]{:S(2)}) collective-permute-start(bf16[128,2176]{1,0:T(8,128)(2,1)S(1)} %concatenate.6), channel_id=1, source_target_pairs={{0,48},{16,0},{32,16},{48,32},{1,49},{17,1},{33,17},{49,33},{2,50}... | collective-permute-start | bytes 1671176 | tf_op jit(solution)/shard_map/ppermute | solution.py:218
  19.2 4.9 %collective-permute-done.1 = bf16[128,2176]{1,0:T(8,128)(2,1)S(1)} collective-permute-done((bf16[128,2176]{1,0:T(8,128)(2,1)S(1)}, bf16[128,2176]{1,0:T(8,128)(2,1)S(1)}, u32[]{:S(2)}, u32[]{:S(2)}) %collective-permute-start.1) | collective-permute-done | bytes 557088 | tf_op jit(solution)/shard_map/ppermute | solution.py:218
  24.2 6.2 %collective-permute-start.2 = (bf16[64,2176]{1,0:T(8,128)(2,1)S(1)}, bf16[64,2176]{1,0:T(8,128)(2,1)S(1)}, u32[]{:S(2)}, u32[]{:S(2)}) collective-permute-start(bf16[64,2176]{1,0:T(8,128)(2,1)S(1)} %slice.29), channel_id=1, source_target_pairs={{0,16},{16,32},{32,48},{48,0},{1,17},{17,33},{33,49},{49,1},{2,18}... | collective-permute-start | bytes 835592 | tf_op jit(solution)/shard_map/ppermute | solution.py:218
  30.4 0.0 collective-permute-done
  30.5 4.2 %collective-permute-start.3 = (bf16[64,2176]{1,0:T(8,128)(2,1)S(1)}, bf16[64,2176]{1,0:T(8,128)(2,1)S(1)}, u32[]{:S(2)}, u32[]{:S(2)}) collective-permute-start(bf16[64,2176]{1,0:T(8,128)(2,1)S(1)} %slice.30), channel_id=1, source_target_pairs={{0,48},{16,0},{32,16},{48,32},{1,49},{17,1},{33,17},{49,33},{2,50}... | collective-permute-start | bytes 835592 | tf_op jit(solution)/shard_map/ppermute | solution.py:218
  34.6 0.1 constant_dynamic-update-slice_fusion.3
  34.7 2.2 collective-permute-done.2
  37.0 2.0 collective-permute-done.3
  39.0 0.1 constant_dynamic-update-slice_fusion.own_ref
  39.1 5.6 %collective-permute-start.4 = (bf16[512,2176]{1,0:T(8,128)(2,1)S(1)}, bf16[512,2176]{1,0:T(8,128)(2,1)}, u32[]{:S(2)}, u32[]{:S(2)}) collective-permute-start(bf16[512,2176]{1,0:T(8,128)(2,1)S(1)} %constant_dynamic-update-slice_fusion.own_ref), channel_id=1, source_target_pairs={{0,1},{1,0},{2,3},{3,2},{4,5},{5,4},{6,7},{7,6},{8,9},{9,8},{10,11... | collective-permute-start | bytes 6684680 | tf_op jit(solution)/shard_map/ppermute | solution.py:218
  44.7 0.1 pad_add_fusion.first_ref
  44.8 4.0 %collective-permute-done.4.other_ref = bf16[512,2176]{1,0:T(8,128)(2,1)} collective-permute-done((bf16[512,2176]{1,0:T(8,128)(2,1)S(1)}, bf16[512,2176]{1,0:T(8,128)(2,1)}, u32[]{:S(2)}, u32[]{:S(2)}) %collective-permute-start.4) | collective-permute-done | bytes 2228256 | tf_op jit(solution)/shard_map/ppermute | solution.py:218
  48.8 5.0 %shard_map.94 = (bf16[14,8,16,2176]{3,2,1,0:T(8,128)(2,1)S(1)}, bf16[8,224,128]{2,1,0:T(8,128)(2,1)S(1)}, s32[43]{0:T(128)S(1)}) custom-call(s32[3]{0:T(128)S(1)} %pad_add_fusion.first_ref, bf16[512,2176]{1,0:T(8,128)(2,1)S(1)} %constant_dynamic-update-slice_fusion.own_ref, bf16[512,2176]{1,0:T(8,128)(2,1)} %collective-permute-done.4.other_ref), custom_call_target="tpu_custom_call" | custom-call | flops 998244352 | bytes 18000000 | tf_op jit(solution)/shard_map/pallas_call | solution.py:172
  53.8 0.0 copy-start
  53.8 3.1 %copy-done = bf16[14,8,16,2176]{3,2,1,0:T(8,128)(2,1)} copy-done((bf16[14,8,16,2176]{3,2,1,0:T(8,128)(2,1)}, bf16[14,8,16,2176]{3,2,1,0:T(8,128)(2,1)S(1)}, u32[]{:S(2)}) %copy-start) | copy-done | bytes 7798808
  57.0 109.7 %all-gather.3.cloned.1.call-done = bf16[8192,1152]{1,0:T(8,128)(2,1)} async-done(((bf16[128,1152]{1,0:T(8,128)(2,1)}), bf16[8192,1152]{1,0:T(8,128)(2,1)}) %all-gather.3.cloned.1.call-update) | async-done | bytes 18874384 | tf_op jit(solution)/shard_map/all_gather | solution.py:262
  166.7 17.3 %shard_map.96 = (bf16[512,2176]{1,0:T(8,128)(2,1)S(1)}, bf16[512,2176]{1,0:T(8,128)(2,1)S(1)}) custom-call(s32[3]{0:T(128)S(1)} %pad_add_fusion.first_ref, s32[43]{0:T(128)S(1)} %get-tuple-element.8.table_ref, bf16[14,8,16,2176]{3,2,1,0:T(8,128)(2,1)} %copy-done, bf16[14,8,16,2176]{3,2,1,0:T(8,128)(2,1)} %copy-done, ...), custom_call_target="tpu_custom_call" | custom-call | flops 8455716864 | bytes 36000000 | tf_op jit(solution)/shard_map/pallas_call | solution.py:194
  184.0 2.6 %collective-permute-start.5 = (bf16[512,2176]{1,0:T(8,128)(2,1)S(1)}, bf16[512,2176]{1,0:T(8,128)(2,1)S(1)}, u32[]{:S(2)}, u32[]{:S(2)}) collective-permute-start(bf16[512,2176]{1,0:T(8,128)(2,1)S(1)} %get-tuple-element.12), channel_id=1, source_target_pairs={{0,1},{1,0},{2,3},{3,2},{4,5},{5,4},{6,7},{7,6},{8,9},{9,8},{10,11... | collective-permute-start | bytes 6684680 | tf_op jit(solution)/shard_map/ppermute | solution.py:218
  186.6 4.0 %collective-permute-done.5 = bf16[512,2176]{1,0:T(8,128)(2,1)S(1)} collective-permute-done((bf16[512,2176]{1,0:T(8,128)(2,1)S(1)}, bf16[512,2176]{1,0:T(8,128)(2,1)S(1)}, u32[]{:S(2)}, u32[]{:S(2)}) %collective-permute-start.5) | collective-permute-done | bytes 2228256 | tf_op jit(solution)/shard_map/ppermute | solution.py:218
  190.5 0.5 add_convert_fusion
  191.0 34.8 %all_to_all.5 = bf16[4,128,2176]{2,1,0:T(8,128)(2,1)S(1)} all-to-all(bf16[4,128,2176]{2,1,0:T(8,128)(2,1)S(1)} %bitcast.5), channel_id=1, replica_groups=mesh['dp'=8,'x'=4,'y'=8,'core'=2] {'x'}, dimensions={0} | all-to-all | bytes 4456448 | tf_op jit(solution)/shard_map/all_to_all | solution.py:236
  225.8 0.3 convert_reduce_fusion
  226.1 0.1 slice_add_fusion
  226.2 0.1 convert.4
  226.3 0.7 copy.18
  227.0 0.9 fusion
  (6 shorter events, 0.1 us)
Async XLA Ops:
  7.2 159.5 %all-gather.3.cloned.1.call-start = ((), (), s32[]{:S(2)}) async-start(), calls=%async_computation.1 | async-start | bytes 19169280 | tf_op jit(solution)/shard_map/all_gather | solution.py:262
  12.0 12.1 %collective-permute-start.1 = (bf16[128,2176]{1,0:T(8,128)(2,1)S(1)}, bf16[128,2176]{1,0:T(8,128)(2,1)S(1)}, u32[]{:S(2)}, u32[]{:S(2)}) collective-permute-start(bf16[128,2176]{1,0:T(8,128)(2,1)S(1)} %concatenate.6), channel_id=1, source_target_pairs={{0,16},{16,32},{32,48},{48,0},{1,17},{17,33},{33,49},{49,1},{2,18}... | collective-permute-start | bytes 1671176 | tf_op jit(solution)/shard_map/ppermute | solution.py:218
  16.0 14.4 %collective-permute-start = (bf16[128,2176]{1,0:T(8,128)(2,1)S(1)}, bf16[128,2176]{1,0:T(8,128)(2,1)S(1)}, u32[]{:S(2)}, u32[]{:S(2)}) collective-permute-start(bf16[128,2176]{1,0:T(8,128)(2,1)S(1)} %concatenate.6), channel_id=1, source_target_pairs={{0,48},{16,0},{32,16},{48,32},{1,49},{17,1},{33,17},{49,33},{2,50}... | collective-permute-start | bytes 1671176 | tf_op jit(solution)/shard_map/ppermute | solution.py:218
  24.2 12.8 %collective-permute-start.2 = (bf16[64,2176]{1,0:T(8,128)(2,1)S(1)}, bf16[64,2176]{1,0:T(8,128)(2,1)S(1)}, u32[]{:S(2)}, u32[]{:S(2)}) collective-permute-start(bf16[64,2176]{1,0:T(8,128)(2,1)S(1)} %slice.29), channel_id=1, source_target_pairs={{0,16},{16,32},{32,48},{48,0},{1,17},{17,33},{33,49},{49,1},{2,18}... | collective-permute-start | bytes 835592 | tf_op jit(solution)/shard_map/ppermute | solution.py:218
  30.5 8.6 %collective-permute-start.3 = (bf16[64,2176]{1,0:T(8,128)(2,1)S(1)}, bf16[64,2176]{1,0:T(8,128)(2,1)S(1)}, u32[]{:S(2)}, u32[]{:S(2)}) collective-permute-start(bf16[64,2176]{1,0:T(8,128)(2,1)S(1)} %slice.30), channel_id=1, source_target_pairs={{0,48},{16,0},{32,16},{48,32},{1,49},{17,1},{33,17},{49,33},{2,50}... | collective-permute-start | bytes 835592 | tf_op jit(solution)/shard_map/ppermute | solution.py:218
  39.1 9.7 %collective-permute-start.4 = (bf16[512,2176]{1,0:T(8,128)(2,1)S(1)}, bf16[512,2176]{1,0:T(8,128)(2,1)}, u32[]{:S(2)}, u32[]{:S(2)}) collective-permute-start(bf16[512,2176]{1,0:T(8,128)(2,1)S(1)} %constant_dynamic-update-slice_fusion.own_ref), channel_id=1, source_target_pairs={{0,1},{1,0},{2,3},{3,2},{4,5},{5,4},{6,7},{7,6},{8,9},{9,8},{10,11... | collective-permute-start | bytes 6684680 | tf_op jit(solution)/shard_map/ppermute | solution.py:218
  53.8 3.2 %copy-start = (bf16[14,8,16,2176]{3,2,1,0:T(8,128)(2,1)}, bf16[14,8,16,2176]{3,2,1,0:T(8,128)(2,1)S(1)}, u32[]{:S(2)}) copy-start(bf16[14,8,16,2176]{3,2,1,0:T(8,128)(2,1)S(1)} %get-tuple-element.9.rows_ref.next_ref) | copy-start | bytes 23396356
  184.0 6.5 %collective-permute-start.5 = (bf16[512,2176]{1,0:T(8,128)(2,1)S(1)}, bf16[512,2176]{1,0:T(8,128)(2,1)S(1)}, u32[]{:S(2)}, u32[]{:S(2)}) collective-permute-start(bf16[512,2176]{1,0:T(8,128)(2,1)S(1)} %get-tuple-element.12), channel_id=1, source_target_pairs={{0,1},{1,0},{2,3},{3,2},{4,5},{5,4},{6,7},{7,6},{8,9},{9,8},{10,11... | collective-permute-start | bytes 6684680 | tf_op jit(solution)/shard_map/ppermute | solution.py:218
Sparse Core Ops, SparseCore 0:
  11.0 155.6 all-gather.2

commit v6 on v4

--- a/solution.py
+++ b/solution.py
@@ -153,7 +153,7 @@
             jax.ShapeDtypeStruct((CHUNKS + 1,), jnp.int32),
         ],
         scratch_shapes=[pltpu.VMEM((blocks, local, SIZE), F32)],
-        compiler_params=pltpu.CompilerParams(vmem_limit_bytes=40 * 1024 * 1024),
+        compiler_params=pltpu.CompilerParams(vmem_limit_bytes=24 * 1024 * 1024),
         cost_estimate=pl.CostEstimate(
             flops=2 * 2 * half * CHUNKS * SLOTS * wide, bytes_accessed=18_000_000, transcendentals=0
         ),
@@ -179,7 +179,7 @@
             scratch_shapes=[pltpu.VMEM(rows.shape, BF)],
         ),
         out_shape=[jax.ShapeDtypeStruct((half, wide), BF)] * 2,
-        compiler_params=pltpu.CompilerParams(vmem_limit_bytes=48 * 1024 * 1024),
+        compiler_params=pltpu.CompilerParams(vmem_limit_bytes=30 * 1024 * 1024),
         cost_estimate=pl.CostEstimate(
             flops=2 * 2 * CHUNKS * SIZE * 1024 * hidden, bytes_accessed=36_000_000, transcendentals=0
         ),

time: 237 us -> 238 us (level)
  local copies, waits for them, and re-layouts: 6.51 us -> 9.72 us
    unnamed x7 -> x9, local copies, waits for them, and re-layouts: 3.96 us -> 7.17 us
where the time goes in v6:
time: 238 us; the launch traced here: 236 us
  waiting for transfers between devices  128 us (54%)
  blocking collectives  34.2 us (14%)
  starting transfers between devices  25.8 us (11%)
  Pallas kernels  22 us (9%)
  between operations  14.2 us (6%)
  local copies, waits for them, and re-layouts  9.72 us (4%)
  other arithmetic  2.52 us (1%)
    all_gather x1, waiting for transfers between devices, on_device(): weights = lax.all_gather(shard, ('dp', 'y'), axis=0)  110 us
    all_to_all x1, blocking collectives, sum_group(): parts = lax.all_to_all(total, 'x', 0, 0, tiled=True)  34.2 us
    ppermute x6, starting transfers between devices, shift(): lax.ppermute(array, axis, [(i, (i + by) % size) for i in range(size)])  25.7 us
    ppermute x6, waiting for transfers between devices, shift(): lax.ppermute(array, axis, [(i, (i + by) % size) for i in range(size)])  17.2 us
    pallas_call x1, Pallas kernels, experts(): pl.pallas_call(functools.partial(experts_kernel, topk), grid_spec=pltpu.P...  15.9 us
    unnamed x9, local copies, waits for them, and re-layouts  7.17 us
  transfers between devices with their start and end apart: 7, of which 6 were waited for; matrix products, arithmetic and copies ran while one was open for 1% of the time, Pallas kernels for 2%

profile of v6, /device:TPU:1, one launch (start us, length us, event | category | flops | bytes accessed | tf_op | source)
XLA Modules:
  0.0 235.9 jit_solution(5384398961183591364)
XLA Ops:
  7.2 0.0 all-gather.3.cloned.1.call-start
  7.2 1.7 shard_map.95
  8.9 0.0 all-gather.3.cloned.1.call-update
  9.0 0.7 convert_element_type.26
  9.7 0.8 subtract_convert_fusion
  10.4 0.1 copy.17
  10.6 0.1 copy.15
  10.7 0.1 copy.16
  10.8 1.2 concatenate.6
  12.0 3.9 %collective-permute-start.1 = (bf16[128,2176]{1,0:T(8,128)(2,1)S(1)}, bf16[128,2176]{1,0:T(8,128)(2,1)S(1)}, u32[]{:S(2)}, u32[]{:S(2)}) collective-permute-start(bf16[128,2176]{1,0:T(8,128)(2,1)S(1)} %concatenate.6), channel_id=1, source_target_pairs={{0,16},{16,32},{32,48},{48,0},{1,17},{17,33},{33,49},{49,1},{2,18}... | collective-permute-start | bytes 1671176 | tf_op jit(solution)/shard_map/ppermute | solution.py:191
  16.0 3.2 %collective-permute-start = (bf16[128,2176]{1,0:T(8,128)(2,1)S(1)}, bf16[128,2176]{1,0:T(8,128)(2,1)S(1)}, u32[]{:S(2)}, u32[]{:S(2)}) collective-permute-start(bf16[128,2176]{1,0:T(8,128)(2,1)S(1)} %concatenate.6), channel_id=1, source_target_pairs={{0,48},{16,0},{32,16},{48,32},{1,49},{17,1},{33,17},{49,33},{2,50}... | collective-permute-start | bytes 1671176 | tf_op jit(solution)/shard_map/ppermute | solution.py:191
  19.2 4.9 %collective-permute-done.1 = bf16[128,2176]{1,0:T(8,128)(2,1)S(1)} collective-permute-done((bf16[128,2176]{1,0:T(8,128)(2,1)S(1)}, bf16[128,2176]{1,0:T(8,128)(2,1)S(1)}, u32[]{:S(2)}, u32[]{:S(2)}) %collective-permute-start.1) | collective-permute-done | bytes 557088 | tf_op jit(solution)/shard_map/ppermute | solution.py:191
  24.2 6.2 %collective-permute-start.2 = (bf16[64,2176]{1,0:T(8,128)(2,1)S(1)}, bf16[64,2176]{1,0:T(8,128)(2,1)S(1)}, u32[]{:S(2)}, u32[]{:S(2)}) collective-permute-start(bf16[64,2176]{1,0:T(8,128)(2,1)S(1)} %slice.29), channel_id=1, source_target_pairs={{0,16},{16,32},{32,48},{48,0},{1,17},{17,33},{33,49},{49,1},{2,18}... | collective-permute-start | bytes 835592 | tf_op jit(solution)/shard_map/ppermute | solution.py:191
  30.4 0.0 collective-permute-done
  30.5 4.2 %collective-permute-start.3 = (bf16[64,2176]{1,0:T(8,128)(2,1)S(1)}, bf16[64,2176]{1,0:T(8,128)(2,1)S(1)}, u32[]{:S(2)}, u32[]{:S(2)}) collective-permute-start(bf16[64,2176]{1,0:T(8,128)(2,1)S(1)} %slice.30), channel_id=1, source_target_pairs={{0,48},{16,0},{32,16},{48,32},{1,49},{17,1},{33,17},{49,33},{2,50}... | collective-permute-start | bytes 835592 | tf_op jit(solution)/shard_map/ppermute | solution.py:191
  34.6 0.1 constant_dynamic-update-slice_fusion.3
  34.7 2.2 collective-permute-done.2
  37.0 2.0 collective-permute-done.3
  39.0 0.1 constant_dynamic-update-slice_fusion.own_ref
  39.1 5.6 %collective-permute-start.4 = (bf16[512,2176]{1,0:T(8,128)(2,1)S(1)}, bf16[512,2176]{1,0:T(8,128)(2,1)}, u32[]{:S(2)}, u32[]{:S(2)}) collective-permute-start(bf16[512,2176]{1,0:T(8,128)(2,1)S(1)} %constant_dynamic-update-slice_fusion.own_ref), channel_id=1, source_target_pairs={{0,1},{1,0},{2,3},{3,2},{4,5},{5,4},{6,7},{7,6},{8,9},{9,8},{10,11... | collective-permute-start | bytes 6684680 | tf_op jit(solution)/shard_map/ppermute | solution.py:191
  44.7 0.1 pad_add_fusion.first_ref
  44.8 4.0 %collective-permute-done.4.other_ref = bf16[512,2176]{1,0:T(8,128)(2,1)} collective-permute-done((bf16[512,2176]{1,0:T(8,128)(2,1)S(1)}, bf16[512,2176]{1,0:T(8,128)(2,1)}, u32[]{:S(2)}, u32[]{:S(2)}) %collective-permute-start.4) | collective-permute-done | bytes 2228256 | tf_op jit(solution)/shard_map/ppermute | solution.py:191
  48.8 4.4 %shard_map.94 = (bf16[14,8,16,2176]{3,2,1,0:T(8,128)(2,1)S(1)}, bf16[8,224,128]{2,1,0:T(8,128)(2,1)S(1)}, s32[15]{0:T(128)S(1)}) custom-call(s32[3]{0:T(128)S(1)} %pad_add_fusion.first_ref, bf16[512,2176]{1,0:T(8,128)(2,1)S(1)} %constant_dynamic-update-slice_fusion.own_ref, bf16[512,2176]{1,0:T(8,128)(2,1)} %collective-permute-done.4.other_ref), custom_call_target="tpu_custom_call" | custom-call | flops 998244352 | bytes 18000000 | tf_op jit(solution)/shard_map/pallas_call | solution.py:146
  53.2 0.0 copy-start
  53.2 3.1 %copy-done = bf16[14,8,16,2176]{3,2,1,0:T(8,128)(2,1)} copy-done((bf16[14,8,16,2176]{3,2,1,0:T(8,128)(2,1)}, bf16[14,8,16,2176]{3,2,1,0:T(8,128)(2,1)S(1)}, u32[]{:S(2)}) %copy-start) | copy-done | bytes 7798808
  56.4 110.3 %all-gather.3.cloned.1.call-done = bf16[8192,1152]{1,0:T(8,128)(2,1)} async-done(((bf16[128,1152]{1,0:T(8,128)(2,1)}), bf16[8192,1152]{1,0:T(8,128)(2,1)}) %all-gather.3.cloned.1.call-update) | async-done | bytes 18874384 | tf_op jit(solution)/shard_map/all_gather | solution.py:235
  166.7 0.0 copy-start.1
  166.7 3.2 %copy-done.1 = bf16[14,8,16,2176]{3,2,1,0:T(8,128)(2,1)S(1)} copy-done((bf16[14,8,16,2176]{3,2,1,0:T(8,128)(2,1)S(1)}, bf16[14,8,16,2176]{3,2,1,0:T(8,128)(2,1)}, u32[]{:S(2)}) %copy-start.1) | copy-done | bytes 7798808
  169.9 15.9 %shard_map.96 = (bf16[512,2176]{1,0:T(8,128)(2,1)S(1)}, bf16[512,2176]{1,0:T(8,128)(2,1)S(1)}) custom-call(s32[3]{0:T(128)S(1)} %pad_add_fusion.first_ref, s32[15]{0:T(128)S(1)} %get-tuple-element.8.table_ref, bf16[14,8,16,2176]{3,2,1,0:T(8,128)(2,1)S(1)} %copy-done.1, bf16[8,224,128]{2,1,0:T(8,128)(2,1)S(1)} %get-tuple-element.10.pick_ref, ...), custom_call_target="tpu_custom_call" | custom-call | flops 8455716864 | bytes 36000000 | tf_op jit(solution)/shard_map/pallas_call | solution.py:168
  185.8 2.6 %collective-permute-start.5 = (bf16[512,2176]{1,0:T(8,128)(2,1)S(1)}, bf16[512,2176]{1,0:T(8,128)(2,1)S(1)}, u32[]{:S(2)}, u32[]{:S(2)}) collective-permute-start(bf16[512,2176]{1,0:T(8,128)(2,1)S(1)} %get-tuple-element.12), channel_id=1, source_target_pairs={{0,1},{1,0},{2,3},{3,2},{4,5},{5,4},{6,7},{7,6},{8,9},{9,8},{10,11... | collective-permute-start | bytes 6684680 | tf_op jit(solution)/shard_map/ppermute | solution.py:191
  188.4 4.0 %collective-permute-done.5 = bf16[512,2176]{1,0:T(8,128)(2,1)S(1)} collective-permute-done((bf16[512,2176]{1,0:T(8,128)(2,1)S(1)}, bf16[512,2176]{1,0:T(8,128)(2,1)S(1)}, u32[]{:S(2)}, u32[]{:S(2)}) %collective-permute-start.5) | collective-permute-done | bytes 2228256 | tf_op jit(solution)/shard_map/ppermute | solution.py:191
  192.3 0.5 add_convert_fusion
  192.8 34.2 %all_to_all.5 = bf16[4,128,2176]{2,1,0:T(8,128)(2,1)S(1)} all-to-all(bf16[4,128,2176]{2,1,0:T(8,128)(2,1)S(1)} %bitcast.4), channel_id=1, replica_groups=mesh['dp'=8,'x'=4,'y'=8,'core'=2] {'x'}, dimensions={0} | all-to-all | bytes 4456448 | tf_op jit(solution)/shard_map/all_to_all | solution.py:209
  227.0 0.3 convert_reduce_fusion
  227.4 0.1 slice_add_fusion
  227.4 0.1 convert.4
  227.5 0.7 copy.18
  228.2 0.9 fusion
  (6 shorter events, 0.1 us)
Async XLA Ops:
  7.2 159.5 %all-gather.3.cloned.1.call-start = ((), (), s32[]{:S(2)}) async-start(), calls=%async_computation.1 | async-start | bytes 19169280 | tf_op jit(solution)/shard_map/all_gather | solution.py:235
  12.0 12.1 %collective-permute-start.1 = (bf16[128,2176]{1,0:T(8,128)(2,1)S(1)}, bf16[128,2176]{1,0:T(8,128)(2,1)S(1)}, u32[]{:S(2)}, u32[]{:S(2)}) collective-permute-start(bf16[128,2176]{1,0:T(8,128)(2,1)S(1)} %concatenate.6), channel_id=1, source_target_pairs={{0,16},{16,32},{32,48},{48,0},{1,17},{17,33},{33,49},{49,1},{2,18}... | collective-permute-start | bytes 1671176 | tf_op jit(solution)/shard_map/ppermute | solution.py:191
  16.0 14.4 %collective-permute-start = (bf16[128,2176]{1,0:T(8,128)(2,1)S(1)}, bf16[128,2176]{1,0:T(8,128)(2,1)S(1)}, u32[]{:S(2)}, u32[]{:S(2)}) collective-permute-start(bf16[128,2176]{1,0:T(8,128)(2,1)S(1)} %concatenate.6), channel_id=1, source_target_pairs={{0,48},{16,0},{32,16},{48,32},{1,49},{17,1},{33,17},{49,33},{2,50}... | collective-permute-start | bytes 1671176 | tf_op jit(solution)/shard_map/ppermute | solution.py:191
  24.2 12.8 %collective-permute-start.2 = (bf16[64,2176]{1,0:T(8,128)(2,1)S(1)}, bf16[64,2176]{1,0:T(8,128)(2,1)S(1)}, u32[]{:S(2)}, u32[]{:S(2)}) collective-permute-start(bf16[64,2176]{1,0:T(8,128)(2,1)S(1)} %slice.29), channel_id=1, source_target_pairs={{0,16},{16,32},{32,48},{48,0},{1,17},{17,33},{33,49},{49,1},{2,18}... | collective-permute-start | bytes 835592 | tf_op jit(solution)/shard_map/ppermute | solution.py:191
  30.5 8.6 %collective-permute-start.3 = (bf16[64,2176]{1,0:T(8,128)(2,1)S(1)}, bf16[64,2176]{1,0:T(8,128)(2,1)S(1)}, u32[]{:S(2)}, u32[]{:S(2)}) collective-permute-start(bf16[64,2176]{1,0:T(8,128)(2,1)S(1)} %slice.30), channel_id=1, source_target_pairs={{0,48},{16,0},{32,16},{48,32},{1,49},{17,1},{33,17},{49,33},{2,50}... | collective-permute-start | bytes 835592 | tf_op jit(solution)/shard_map/ppermute | solution.py:191
  39.1 9.7 %collective-permute-start.4 = (bf16[512,2176]{1,0:T(8,128)(2,1)S(1)}, bf16[512,2176]{1,0:T(8,128)(2,1)}, u32[]{:S(2)}, u32[]{:S(2)}) collective-permute-start(bf16[512,2176]{1,0:T(8,128)(2,1)S(1)} %constant_dynamic-update-slice_fusion.own_ref), channel_id=1, source_target_pairs={{0,1},{1,0},{2,3},{3,2},{4,5},{5,4},{6,7},{7,6},{8,9},{9,8},{10,11... | collective-permute-start | bytes 6684680 | tf_op jit(solution)/shard_map/ppermute | solution.py:191
  53.2 3.2 %copy-start = (bf16[14,8,16,2176]{3,2,1,0:T(8,128)(2,1)}, bf16[14,8,16,2176]{3,2,1,0:T(8,128)(2,1)S(1)}, u32[]{:S(2)}) copy-start(bf16[14,8,16,2176]{3,2,1,0:T(8,128)(2,1)S(1)} %get-tuple-element.9.rows_ref) | copy-start | bytes 23396356
  166.7 3.2 %copy-start.1 = (bf16[14,8,16,2176]{3,2,1,0:T(8,128)(2,1)S(1)}, bf16[14,8,16,2176]{3,2,1,0:T(8,128)(2,1)}, u32[]{:S(2)}) copy-start(bf16[14,8,16,2176]{3,2,1,0:T(8,128)(2,1)} %copy-done) | copy-start | bytes 23396356
  185.8 6.5 %collective-permute-start.5 = (bf16[512,2176]{1,0:T(8,128)(2,1)S(1)}, bf16[512,2176]{1,0:T(8,128)(2,1)S(1)}, u32[]{:S(2)}, u32[]{:S(2)}) collective-permute-start(bf16[512,2176]{1,0:T(8,128)(2,1)S(1)} %get-tuple-element.12), channel_id=1, source_target_pairs={{0,1},{1,0},{2,3},{3,2},{4,5},{5,4},{6,7},{7,6},{8,9},{9,8},{10,11... | collective-permute-start | bytes 6684680 | tf_op jit(solution)/shard_map/ppermute | solution.py:191
Sparse Core Ops, SparseCore 0:
  11.0 155.6 all-gather.2
